TPU v7x, 512 devices: a whole 4x4x16 slice. The times are simulated.
512 devices in a mesh: lat: 16 (over y_hi, x, core), lon: 32 (over z, y_lo).
Axes of the slice: x: 4, y: 4 (y_hi: 2, y_lo: 2; y = y_hi * 2 + y_lo), z: 16, core: 2. Of those that a mesh axis runs over, the one named last changes fastest.
Arguments:
- grid: bfloat16 [2, 96, 384, 192], P(None, 'lat', 'lon'), may hold values from -6 to 6
- region_ids: int32 [2, 96, 384], P(None, 'lat', 'lon'), may hold values from 1 to 8, as said below
- cotangent: bfloat16 [2, 96, 384, 192], P(None, 'lat', 'lon'), may hold values from -6 to 6
- norm_gain: float32 [2, 192], replicated, may hold values from 0.25 to 1.75
- norm_shift: float32 [2, 192], replicated, may hold values from -1.5 to 1.5
- qkv_weight: bfloat16 [192, 576], replicated, may hold values from -0.4375 to 0.4375
- qkv_bias: float32 [576], replicated, may hold values from -1.5 to 1.5
- proj_weight: bfloat16 [192, 192], replicated, may hold values from -0.4375 to 0.4375
- proj_bias: float32 [192], replicated, may hold values from -1.5 to 1.5
- fc1_weight: bfloat16 [192, 768], replicated, may hold values from -0.4375 to 0.4375
- fc1_bias: float32 [768], replicated, may hold values from -1.5 to 1.5
- fc2_weight: bfloat16 [768, 192], replicated, may hold values from -0.21875 to 0.21875
- fc2_bias: float32 [192], replicated, may hold values from -1.5 to 1.5
- bias_table: float32 [1, 16, 6, 3312], P(None, 'lat'), may hold values from -3 to 400
- pair_index: int32 [144, 144], replicated, may hold values from 0 to 3311
Outputs:
- output: bfloat16 [2, 96, 384, 192], P(None, 'lat', 'lon')
- grid_grad: bfloat16 [2, 96, 384, 192], P(None, 'lat', 'lon')
- norm_gain_grad: float32 [2, 192], replicated
- norm_shift_grad: float32 [2, 192], replicated
- qkv_weight_grad: float32 [192, 576], replicated
- qkv_bias_grad: float32 [576], replicated
- proj_weight_grad: float32 [192, 192], replicated
- proj_bias_grad: float32 [192], replicated
- fc1_weight_grad: float32 [192, 768], replicated
- fc1_bias_grad: float32 [768], replicated
- fc2_weight_grad: float32 [768, 192], replicated
- fc2_bias_grad: float32 [192], replicated
- table_grad: float32 [1, 16, 6, 3312], P(None, 'lat')
Inputs may be any that keep to these rules, and one draw needn't show every extreme that they name: `region_ids`: labels depend on level and latitude row only, not on longitude.
All inputs are finite; a program needn't handle non-finite values.
Results may differ from a plain program's by a relative error of at most 0.018.
Values may be sent and summed in bfloat16 or wider, within the bound.
A program may use at most 64 MiB of HBM per device.

v0:
```python
import math

import jax
import jax.numpy as jnp
from jax import lax
from jax.sharding import PartitionSpec as P

WZ = 2
WLAT = 6
WLON = 12
NBIAS = 3312


NEG_FILL = -1e30
NORM_EPS = 1e-05
ROOT_HALF = 1.0 / math.sqrt(2.0)
ROOT_TWOPI = 1.0 / math.sqrt(2.0 * math.pi)


def passed_along(block, axis, distance):
    devices = range(lax.axis_size(axis))
    route = [((i - distance) % len(devices), i) for i in devices]
    return lax.ppermute(block, axis, route)


def mixing(form, left_op, right_op):
    return jnp.einsum(form, left_op, right_op, preferred_element_type=jnp.float32)


def layer_norm(values, gain_row, shift_row):
    centred = values - jnp.mean(values, -1, keepdims=True)
    inv_std = lax.rsqrt(jnp.mean(centred * centred, -1, keepdims=True) + NORM_EPS)
    normed = centred * inv_std
    return (normed * gain_row + shift_row, normed, inv_std)


def norm_back(incoming, normed, inv_std, gain_row):
    scaled = incoming * gain_row
    outgoing = inv_std * (
        scaled
        - jnp.mean(scaled, -1, keepdims=True)
        - normed * jnp.mean(scaled * normed, -1, keepdims=True)
    )
    return (outgoing, jnp.sum(incoming * normed, 0), jnp.sum(incoming, 0))


def to_windows(field):
    levels, lat_rows, lon_cols = field.shape[:3]
    trailing = field.shape[3:]
    shaped = field.reshape(
        (levels // WZ, WZ, lat_rows // WLAT, WLAT, lon_cols // WLON, WLON) + trailing
    )
    order_axes = (0, 2, 4, 1, 3, 5) + tuple(range(6, 6 + len(trailing)))
    return shaped.transpose(order_axes).reshape(
        (levels // WZ, lat_rows // WLAT, lon_cols // WLON, WZ * WLAT * WLON) + trailing
    )


def from_windows(windows, levels, lat_rows, lon_cols):
    channels = windows.shape[-1]
    shaped = windows.reshape(
        levels // WZ, lat_rows // WLAT, lon_cols // WLON, WZ, WLAT, WLON, channels
    )
    return shaped.transpose(0, 3, 1, 4, 2, 5, 6).reshape(levels, lat_rows, lon_cols, channels)


def attention_forward(inputs, window_ids, pair_bias, params):
    channels = inputs.shape[-1]
    num_heads = pair_bias.shape[2]
    head_size = channels // num_heads
    flat_in = inputs.reshape(-1, channels).astype(jnp.float32)
    normed_in, hat_one, inv_one = layer_norm(flat_in, params[0][0], params[1][0])
    first_b = normed_in.astype(jnp.bfloat16)
    triple = (jnp.dot(first_b, params[2], preferred_element_type=jnp.float32) + params[3]).astype(
        jnp.bfloat16
    )
    triple = triple.reshape(inputs.shape[:4] + (3, num_heads, head_size))
    queries = triple[:, :, :, :, 0]
    keys_b = triple[:, :, :, :, 1]
    values_b = triple[:, :, :, :, 2]
    scores = (
        mixing("xyzihd,xyzjhd->xyzhij", queries, keys_b) * head_size ** (-0.5)
        + pair_bias[:, :, None]
    )
    allowed = (window_ids[..., :, None] == window_ids[..., None, :])[:, :, :, None]
    scores = jnp.where(allowed, scores, NEG_FILL)
    weights = jnp.exp(scores - jnp.max(scores, -1, keepdims=True))
    softmax_f = weights / jnp.sum(weights, -1, keepdims=True)
    softmax_b = softmax_f.astype(jnp.bfloat16)
    mixed_b = (
        mixing("xyzhij,xyzjhd->xyzihd", softmax_b, values_b)
        .astype(jnp.bfloat16)
        .reshape(-1, channels)
    )
    attended = flat_in + jnp.dot(mixed_b, params[4], preferred_element_type=jnp.float32) + params[5]
    return (
        attended,
        (hat_one, inv_one, first_b, queries, keys_b, values_b, softmax_f, softmax_b, mixed_b),
    )


def mlp_forward(attended, params):
    normed_two, hat_two, inv_two = layer_norm(attended, params[0][1], params[1][1])
    second_b = normed_two.astype(jnp.bfloat16)
    hidden = jnp.dot(second_b, params[6], preferred_element_type=jnp.float32) + params[7]
    cumul = 0.5 * (1.0 + lax.erf(hidden * ROOT_HALF))
    active_b = (hidden * cumul).astype(jnp.bfloat16)
    result = (
        attended + jnp.dot(active_b, params[8], preferred_element_type=jnp.float32) + params[9]
    ).astype(jnp.bfloat16)
    return (result, (hat_two, inv_two, second_b, hidden, cumul, active_b))


def mlp_backward(incoming_b, saved, params):
    hat_two, inv_two, second_b, hidden, cumul, active_b = saved
    grad_out = incoming_b.astype(jnp.float32)
    fc2_w_grad = jnp.dot(active_b.T, incoming_b, preferred_element_type=jnp.float32)
    fc2_b_grad = jnp.sum(grad_out, 0)
    d_active = jnp.dot(incoming_b, params[8].T, preferred_element_type=jnp.float32)
    d_hidden = d_active * (cumul + hidden * jnp.exp(-0.5 * hidden * hidden) * ROOT_TWOPI)
    d_hidden_b = d_hidden.astype(jnp.bfloat16)
    fc1_w_grad = jnp.dot(second_b.T, d_hidden_b, preferred_element_type=jnp.float32)
    fc1_b_grad = jnp.sum(d_hidden, 0)
    d_second = jnp.dot(d_hidden_b, params[6].T, preferred_element_type=jnp.float32)
    back_two, gain_two, shift_two = norm_back(d_second, hat_two, inv_two, params[0][1])
    return (
        grad_out + back_two,
        (fc1_w_grad, fc1_b_grad, fc2_w_grad, fc2_b_grad),
        gain_two,
        shift_two,
    )


def attention_backward(d_attended, saved, params):
    hat_one, inv_one, first_b, queries, keys_b, values_b, softmax_f, softmax_b, mixed_b = saved
    head_size = queries.shape[-1]
    d_att_b = d_attended.astype(jnp.bfloat16)
    proj_w_grad = jnp.dot(mixed_b.T, d_att_b, preferred_element_type=jnp.float32)
    proj_b_grad = jnp.sum(d_attended, 0)
    d_mixed = (
        jnp.dot(d_att_b, params[4].T, preferred_element_type=jnp.float32)
        .astype(jnp.bfloat16)
        .reshape(queries.shape)
    )
    d_softmax = mixing("xyzihd,xyzjhd->xyzhij", d_mixed, values_b)
    d_values = mixing("xyzhij,xyzihd->xyzjhd", softmax_b, d_mixed)
    d_scores = softmax_f * (d_softmax - jnp.sum(d_softmax * softmax_f, -1, keepdims=True))
    d_pairs = jnp.sum(d_scores, 2)
    d_scaled = (d_scores * head_size ** (-0.5)).astype(jnp.bfloat16)
    d_queries = mixing("xyzhij,xyzjhd->xyzihd", d_scaled, keys_b)
    d_keys = mixing("xyzhij,xyzihd->xyzjhd", d_scaled, queries)
    d_triple = jnp.stack([d_queries, d_keys, d_values], 4).reshape(first_b.shape[0], -1)
    d_triple_b = d_triple.astype(jnp.bfloat16)
    qkv_w_grad = jnp.dot(first_b.T, d_triple_b, preferred_element_type=jnp.float32)
    qkv_b_grad = jnp.sum(d_triple, 0)
    d_first = jnp.dot(d_triple_b, params[2].T, preferred_element_type=jnp.float32)
    back_one, gain_one, shift_one = norm_back(d_first, hat_one, inv_one, params[0][0])
    d_inputs = (d_attended + back_one).astype(jnp.bfloat16)
    return (
        d_inputs,
        (qkv_w_grad, qkv_b_grad, proj_w_grad, proj_b_grad),
        gain_one,
        shift_one,
        d_pairs,
    )


def table_gradient(d_pairs, pair_index):
    zwin, latwin, num_heads = d_pairs.shape[:3]
    flat_terms = d_pairs.reshape(zwin * latwin * num_heads, -1)
    summed = jax.ops.segment_sum(flat_terms.T, pair_index.reshape(-1), num_segments=NBIAS)
    return summed.T.reshape(zwin, latwin, num_heads, NBIAS)


def unroll_field(field):
    lat_rows = field.shape[1]
    lon_cols = field.shape[2]
    field = jnp.roll(field, WZ // 2, 0)
    from_lat = passed_along(field[:, lat_rows - WLAT // 2 :], "lat", 1)
    field = jnp.concatenate([from_lat, field[:, : lat_rows - WLAT // 2]], 1)
    from_lon = passed_along(field[:, :, lon_cols - WLON // 2 :], "lon", 1)
    return jnp.concatenate([from_lon, field[:, :, : lon_cols - WLON // 2]], 2)


def on_device(
    grid,
    region_ids,
    cotangent,
    norm_gain,
    norm_shift,
    qkv_weight,
    qkv_bias,
    proj_weight,
    proj_bias,
    fc1_weight,
    fc1_bias,
    fc2_weight,
    fc2_bias,
    bias_table,
    pair_index,
):
    params = (
        norm_gain,
        norm_shift,
        qkv_weight,
        qkv_bias,
        proj_weight,
        proj_bias,
        fc1_weight,
        fc1_bias,
        fc2_weight,
        fc2_bias,
    )
    levels, lat_rows, lon_cols, channels = grid.shape
    half_lat = WLAT // 2
    half_lon = WLON // 2
    from_lon = passed_along(
        (grid[:, :, :half_lon], cotangent[:, :, :half_lon], region_ids[:, :, :half_lon]), "lon", -1
    )
    grid_cols = jnp.concatenate([grid[:, :, half_lon:], from_lon[0]], 2)
    cot_cols = jnp.concatenate([cotangent[:, :, half_lon:], from_lon[1]], 2)
    ids_cols = jnp.concatenate([region_ids[:, :, half_lon:], from_lon[2]], 2)
    from_lat = passed_along(
        (grid_cols[:, :half_lat], cot_cols[:, :half_lat], ids_cols[:, :half_lat]), "lat", -1
    )
    grid_roll = jnp.roll(jnp.concatenate([grid_cols[:, half_lat:], from_lat[0]], 1), -(WZ // 2), 0)
    cot_roll = jnp.roll(jnp.concatenate([cot_cols[:, half_lat:], from_lat[1]], 1), -(WZ // 2), 0)
    ids_roll = jnp.roll(jnp.concatenate([ids_cols[:, half_lat:], from_lat[2]], 1), -(WZ // 2), 0)
    pair_bias = jnp.take(bias_table, pair_index, axis=3)
    win_grid = to_windows(grid_roll)
    win_ids = to_windows(ids_roll)
    win_cot = to_windows(cot_roll)
    attended, saved_att = attention_forward(win_grid, win_ids, pair_bias, params)
    result, saved_mlp = mlp_forward(attended, params)
    result_roll = from_windows(result.reshape(win_grid.shape), levels, lat_rows, lon_cols)
    output = unroll_field(result_roll)
    d_attended, mlp_grads, gain_two, shift_two = mlp_backward(
        win_cot.reshape(-1, channels), saved_mlp, params
    )
    d_inputs, att_grads, gain_one, shift_one, d_pairs = attention_backward(
        d_attended, saved_att, params
    )
    gain_grad = jnp.stack([gain_one, gain_two])
    shift_grad = jnp.stack([shift_one, shift_two])
    (
        gain_grad,
        shift_grad,
        qkv_w_grad,
        qkv_b_grad,
        proj_w_grad,
        proj_b_grad,
        fc1_w_grad,
        fc1_b_grad,
        fc2_w_grad,
        fc2_b_grad,
    ) = lax.psum(
        (
            gain_grad,
            shift_grad,
            att_grads[0],
            att_grads[1],
            att_grads[2],
            att_grads[3],
            mlp_grads[0],
            mlp_grads[1],
            mlp_grads[2],
            mlp_grads[3],
        ),
        ("lat", "lon"),
    )
    table_grad = lax.psum(table_gradient(d_pairs, pair_index).astype(jnp.bfloat16), "lon").astype(
        jnp.float32
    )
    grad_roll = from_windows(d_inputs.reshape(win_grid.shape), levels, lat_rows, lon_cols)
    grid_grad = unroll_field(grad_roll)
    return (
        output,
        grid_grad,
        gain_grad,
        shift_grad,
        qkv_w_grad,
        qkv_b_grad,
        proj_w_grad,
        proj_b_grad,
        fc1_w_grad,
        fc1_b_grad,
        fc2_w_grad,
        fc2_b_grad,
        table_grad,
    )


def solution(mesh):
    placed = (
        P(None, "lat", "lon", None),
        P(None, "lat", "lon"),
        P(None, "lat", "lon", None),
        P(),
        P(),
        P(),
        P(),
        P(),
        P(),
        P(),
        P(),
        P(),
        P(),
        P(None, "lat", None, None),
        P(),
    )
    return jax.shard_map(
        on_device,
        mesh=mesh,
        in_specs=placed,
        out_specs=(
            P(None, "lat", "lon", None),
            P(None, "lat", "lon", None),
            P(),
            P(),
            P(),
            P(),
            P(),
            P(),
            P(),
            P(),
            P(),
            P(),
            P(None, "lat", None, None),
        ),
        check_vma=False,
    )
```

profile of v0, /device:TPU:1, one launch (start us, length us, event | category | flops | bytes accessed | tf_op | source)
XLA Modules:
  0.0 858.3 jit_solution(4426077277607805708)
XLA Ops:
  7.2 0.8 fusion.52
  8.1 13.0 %collective-permute-start.2 = (s32[2,6,6]{2,0,1:T(2,128)S(1)}, s32[2,6,6]{2,0,1:T(2,128)S(1)}, u32[]{:S(2)}, u32[]{:S(2)}) collective-permute-start(s32[2,6,6]{2,0,1:T(2,128)S(1)} %get-tuple-element.97), channel_id=1, source_target_pairs={{1,0},{2,1},{3,2},{4,3},{5,4},{6,5},{7,6},{8,7},{9,8},{10,9},{11,1... | collective-permute-start | bytes 872 | tf_op jit(solution)/shard_map/ppermute | solution.py:23
  21.0 0.8 fusion.51
  21.9 2.1 collective-permute-start
  24.0 0.8 fusion.48
  24.8 3.6 collective-permute-start.6
  28.5 1.0 compare_and_fusion
  29.4 0.9 compare_select_fusion
  30.4 0.8 fusion.53
  31.3 1.3 fusion.54
  32.6 1.7 reshape.397
  34.5 3.4 collective-permute-start.3
  37.9 1.4 copy.75
  39.4 38.7 %gather_fusion = f32[20736,6]{1,0:T(8,128)} fusion(f32[6,3312]{0,1:T(8,128)S(1)} %bitcast.81, s32[21504]{0:T(1024)S(1)} %pad_clamp_fusion), kind=kCustom, calls=%fused_computation | custom fusion | bytes 1078272 | tf_op jit(solution)/shard_map/jit(_take)/gather | solution.py:229
  78.0 11.6 %copy.77 = f32[144,144,6]{0,1,2:T(8,128)S(1)} copy(f32[144,144,6]{2,1,0:T(8,128)} %bitcast.82) | data formatting | bytes 995328 | tf_op jit(solution)/shard_map/jit(_take)/gather | solution.py:229
  90.0 5.6 collective-permute-start.1
  95.8 3.4 collective-permute-start.7
  101.2 0.8 convert_reduce_fusion
  102.1 0.9 add_convert_fusion
  103.8 0.8 fusion.55
  106.1 1.0 multiply_convert_fusion.1
  107.1 0.9 fusion.57
  108.0 0.9 multiply_reduce_fusion.1
  109.7 0.9 fusion.36
  110.6 1.2 fusion.19
  111.9 1.0 convolution_bitcast_fusion
  113.4 0.8 copy-done.3
  115.6 1.0 fusion.16
  116.5 0.9 copy.88
  117.5 1.1 fusion.59
  119.1 1.9 collective-permute-start.4
  122.4 2.1 collective-permute-start.8
  124.5 1.1 fusion.58
  125.6 6.1 copy.90
  131.8 112.8 %scatter_custom_fusion = f32[3312,6]{1,0:T(8,128)S(1)} fusion(s32[20736]{0:T(1024)} %reshape.397, f32[20736,6]{1,0:T(8,128)} %copy.90, f32[]{:T(128)} %constant.15.clone.1), kind=kCustom, calls=%fused_computation.26 | custom fusion | flops 124416 | bytes 80000 | tf_op jit(solution)/shard_map/scatter-add | solution.py:171
  245.3 100.8 %psum.87 = bf16[1,1,6,3312]{2,3,1,0:T(8,128)(2,1)S(1)} all-reduce(bf16[1,1,6,3312]{2,3,1,0:T(8,128)(2,1)S(1)} %convert_bitcast_fusion), channel_id=1, replica_groups=mesh['lat'=16,'lon'=32] {'lon'}, use_global_device_ids=true, to_apply=%region_30.31 | all-reduce | flops 19872 | bytes 79488 | tf_op jit(solution)/shard_map/psum | solution.py:271
  346.1 1.0 copy.91
  347.1 128.6 %all-reduce = (f32[2,192]{1,0:T(2,128)}, f32[2,192]{1,0:T(2,128)}, f32[576]{0:T(1024)}, f32[192]{0:T(256)}, f32[768]{0:T(1024)}, /*index=5*/f32[192]{0:T(256)}) all-reduce(f32[2,192]{1,0:T(2,128)S(1)} %pad_maximum_fusion.9, f32[2,192]{1,0:T(2,128)S(1)} %pad_maximum_fusion.10, ...), channel_id=1, replica_groups=mesh['lat'=16,'lon'=32] {'lat','lon'}, use_global_device_ids=true, to_apply=%region_13.14 | all-reduce | flops 2496 | bytes 19968 | tf_op jit(solution)/shard_map/psum | solution.py:256
  475.9 3.8 collective-permute-start.5
  480.0 2.3 collective-permute-start.9
  482.8 0.7 pad_maximum_fusion.5
  483.5 3.3 collective-permute-done.9
  486.8 0.7 pad_maximum_fusion.6
  487.6 358.7 %all-reduce.4.cloned.1.call-done = (f32[192,576]{1,0:T(8,128)}, f32[192,192]{1,0:T(8,128)}, f32[192,768]{1,0:T(8,128)}, f32[768,192]{0,1:T(8,128)}) async-done(((f32[192,576]{1,0:T(8,128)}, f32[192,192]{1,0:T(8,128)}, f32[192,768]{1,0:T(8,128)}, f32[768,192]{0,1:T(8,128)}), (f32[192,576]{1,0:T(8,128)}, f32[192,192]{1,0:T(8,128)}, f32[192,768]{1,0:T(8,128)}, ...) | async-done | bytes 1769488 | tf_op jit(solution)/shard_map/psum | solution.py:256
  846.3 1.9 copy.102
  848.2 1.6 copy.103
  849.8 0.8 copy.104
  850.6 0.8 copy.105
  (124 shorter events, 11.2 us)
Async XLA Ops:
  7.2 98.9 %copy-start = (bf16[192,768]{1,0:T(8,128)(2,1)S(1)}, bf16[192,768]{1,0:T(8,128)(2,1)}, u32[]{:S(2)}) copy-start(bf16[192,768]{1,0:T(8,128)(2,1)} %param.24) | copy-start | bytes 884740
  7.2 839.1 %all-reduce.4.cloned.1.call-start = ((), (), s32[]{:S(2)}) async-start(), calls=%async_computation | async-start | bytes 3735552 | tf_op jit(solution)/shard_map/psum | solution.py:256
  8.1 26.3 %collective-permute-start.2 = (s32[2,6,6]{2,0,1:T(2,128)S(1)}, s32[2,6,6]{2,0,1:T(2,128)S(1)}, u32[]{:S(2)}, u32[]{:S(2)}) collective-permute-start(s32[2,6,6]{2,0,1:T(2,128)S(1)} %get-tuple-element.97), channel_id=1, source_target_pairs={{1,0},{2,1},{3,2},{4,3},{5,4},{6,5},{7,6},{8,7},{9,8},{10,9},{11,1... | collective-permute-start | bytes 872 | tf_op jit(solution)/shard_map/ppermute | solution.py:23
  21.9 68.0 %collective-permute-start = (bf16[2,6,6,192]{3,0,2,1:T(2,128)(2,1)S(1)}, bf16[2,6,6,192]{3,0,2,1:T(2,128)(2,1)S(1)}, u32[]{:S(2)}, u32[]{:S(2)}) collective-permute-start(bf16[2,6,6,192]{3,0,2,1:T(2,128)(2,1)S(1)} %get-tuple-element.91), channel_id=1, source_target_pairs={{1,0},{2,1},{3,2},{4,3},{5,4},{6,5},{7,6},{8,7},{9,8},{10,9},{11,1... | collective-permute-start | bytes 82952 | tf_op jit(solution)/shard_map/ppermute | solution.py:23
  24.8 70.8 %collective-permute-start.6 = (bf16[2,6,6,192]{3,0,2,1:T(2,128)(2,1)S(1)}, bf16[2,6,6,192]{3,0,2,1:T(2,128)(2,1)S(1)}, u32[]{:S(2)}, u32[]{:S(2)}) collective-permute-start(bf16[2,6,6,192]{3,0,2,1:T(2,128)(2,1)S(1)} %get-tuple-element.83), channel_id=1, source_target_pairs={{1,0},{2,1},{3,2},{4,3},{5,4},{6,5},{7,6},{8,7},{9,8},{10,9},{11,1... | collective-permute-start | bytes 82952 | tf_op jit(solution)/shard_map/ppermute | solution.py:23
  34.5 55.2 %collective-permute-start.3 = (s32[2,3,12]{2,0,1:T(2,128)S(1)}, s32[2,3,12]{2,0,1:T(2,128)S(1)}, u32[]{:S(2)}, u32[]{:S(2)}) collective-permute-start(s32[2,3,12]{2,0,1:T(2,128)S(1)} %get-tuple-element.93), channel_id=1, source_target_pairs={{32,0},{64,32},{96,64},{128,96},{160,128},{192,160},{224,192},{256... | collective-permute-start | bytes 872 | tf_op jit(solution)/shard_map/ppermute | solution.py:23
  89.7 13.3 %copy-start.4 = (bf16[192,576]{1,0:T(8,128)(2,1)S(1)}, bf16[192,576]{1,0:T(8,128)(2,1)}, u32[]{:S(2)}) copy-start(bf16[192,576]{1,0:T(8,128)(2,1)} %param.20) | copy-start | bytes 663556
  89.7 13.3 %copy-start.15 = (f32[576]{0:T(1024)S(1)}, f32[576]{0:T(1024)}, u32[]{:S(2)}) copy-start(f32[576]{0:T(1024)} %param.21) | copy-start | bytes 6916
  90.0 9.2 %collective-permute-start.1 = (bf16[2,3,12,192]{3,0,2,1:T(2,128)(2,1)S(1)}, bf16[2,3,12,192]{3,0,2,1:T(2,128)(2,1)S(1)}, u32[]{:S(2)}, u32[]{:S(2)}) collective-permute-start(bf16[2,3,12,192]{3,0,2,1:T(2,128)(2,1)S(1)} %get-tuple-element.89), channel_id=1, source_target_pairs={{32,0},{64,32},{96,64},{128,96},{160,128},{192,160},{224,192},{256... | collective-permute-start | bytes 82952 | tf_op jit(solution)/shard_map/ppermute | solution.py:23
  95.8 5.3 collective-permute-start.7
  100.5 2.9 copy-start.12
  103.4 9.5 %copy-start.2 = (bf16[144,576]{0,1:T(8,128)(2,1)}, bf16[144,576]{0,1:T(8,128)(2,1)S(1)}, u32[]{:S(2)}) copy-start(bf16[144,576]{0,1:T(8,128)(2,1)S(1)} %copy.72) | copy-start | bytes 497668
  104.6 0.9 copy-start.9
  104.6 0.9 copy-start.22
  104.6 1.4 copy-start.14
  104.6 1.4 copy-start.16
  105.0 2.1 copy-start.10
  113.2 1.0 copy-start.3
  114.5 0.9 copy-start.6
  114.7 2.8 copy-start.1
  115.4 3.2 copy-start.11
  115.4 3.2 copy-start.23
  117.5 4.2 copy-start.5
  117.5 4.1 copy-start.13
  119.1 356.7 %collective-permute-start.4 = (bf16[2,3,12,192]{3,0,2,1:T(2,128)(2,1)S(1)}, bf16[2,3,12,192]{3,0,2,1:T(2,128)(2,1)S(1)}, u32[]{:S(2)}, u32[]{:S(2)}) collective-permute-start(bf16[2,3,12,192]{3,0,2,1:T(2,128)(2,1)S(1)} %fusion.34), channel_id=1, source_target_pairs={{480,0},{0,32},{32,64},{64,96},{96,128},{128,160},{160,192},{192,2... | collective-permute-start | bytes 82952 | tf_op jit(solution)/shard_map/ppermute | solution.py:23
  122.4 357.4 %collective-permute-start.8 = (bf16[2,3,12,192]{3,0,2,1:T(2,128)(2,1)S(1)}, bf16[2,3,12,192]{3,0,2,1:T(2,128)(2,1)S(1)}, u32[]{:S(2)}, u32[]{:S(2)}) collective-permute-start(bf16[2,3,12,192]{3,0,2,1:T(2,128)(2,1)S(1)} %fusion.32), channel_id=1, source_target_pairs={{480,0},{0,32},{32,64},{64,96},{96,128},{128,160},{160,192},{192,2... | collective-permute-start | bytes 82952 | tf_op jit(solution)/shard_map/ppermute | solution.py:23
  244.6 0.7 copy-start.20
  244.6 0.7 copy-start.19
  346.1 1.0 copy-start.17
  346.1 1.0 copy-start.18
  346.1 1.0 copy-start.21
  475.9 6.8 collective-permute-start.5
  480.0 6.8 collective-permute-start.9
  846.3 3.6 copy-start.8
  846.3 4.4 copy-start.7
Sparse Core Ops, SparseCore 0:
  347.2 499.0 all-reduce.3
where the time goes:
time: 860 us; the launch traced here: 858 us
  waiting for transfers between devices  363 us (42%)
  blocking collectives  229 us (27%)
  other arithmetic  123 us (14%)
  local copies, waits for them, and re-layouts  75.9 us (9%)
  starting transfers between devices  41.3 us (5%)
  between operations  14.8 us (2%)
  matrix products  10.9 us (1%)
    psum x1, waiting for transfers between devices, on_device(): lax.psum((gain_grad, shift_grad, att_grads[0], att_grads[1], att_grads[2]...  359 us
    psum x1, blocking collectives, on_device(): lax.psum((gain_grad, shift_grad, att_grads[0], att_grads[1], att_grads[2]...  129 us
    scatter-add x1, other arithmetic, table_gradient(): jax.ops.segment_sum(flat_terms.T, pair_index.reshape(-1), num_segments=NB...  113 us
    psum x1, blocking collectives, on_device(): lax.psum(table_gradient(d_pairs, pair_index).astype(jnp.bfloat16), 'lon')  101 us
    gather x2, local copies, waits for them, and re-layouts, on_device(): pair_bias = jnp.take(bias_table, pair_index, axis=3)  50.3 us
    ppermute x10, starting transfers between devices, passed_along(): return lax.ppermute(block, axis, route)  41.3 us
  transfers between devices with their start and end apart: 11, of which 4 were waited for; matrix products, arithmetic and copies ran while one was open for 22% of the time, Pallas kernels for 0%

commit v1 on v0

v1 whole, which is shorter than its diff:
```python
import math

import jax
import jax.numpy as jnp
import numpy as np
from jax import lax
from jax.experimental import pallas as pl
from jax.experimental.pallas import tpu as pltpu
from jax.sharding import PartitionSpec as P

F32 = jnp.float32
BF16 = jnp.bfloat16
MESH = pl.DeviceIdType.MESH

C = 192
HEADS = 6
HEAD = 32
FF = 768
TOK = 144
NBIAS = 3312
NHI = 26
NEG_FILL = -1e30
NORM_EPS = 1e-05
ROOT_HALF = 1.0 / math.sqrt(2.0)
ROOT_TWOPI = 1.0 / math.sqrt(2.0 * math.pi)
SCALE = HEAD ** (-0.5)

ROWS = 3584
FC2_ROW = 0
FC1_ROW = 1152
QP_ROW = 2304
SMALL_ROW = 3456
CHUNKS = ((0, 64), (2048, 48))
OWNED = 112
ZROWS = 7


def dot(a, b, ca=1, cb=0):
    return lax.dot_general(a, b, (((ca,), (cb,)), ((), ())), preferred_element_type=F32)


def selectors():
    padded = lambda l, r, q: (l * 6 + r) * 16 + q
    send = np.zeros((144, 192), np.float32)
    gather = np.zeros((144, 336), np.float32)
    send_out = np.zeros((144, 144), np.float32)
    place = np.zeros((192, 288), np.float32)
    for l in range(2):
        for i in range(6):
            for j in range(12):
                tok = l * 72 + i * 12 + j
                lev = (l + 1) % 2
                far_i, far_j = i >= 3, j >= 6
                if not far_i and not far_j:
                    gather[tok, padded(lev, i + 3, j + 6)] = 1
                    place[padded(lev, i + 3, j + 6), tok] = 1
                    continue
                d = 2 if (far_i and far_j) else (1 if far_i else 0)
                m = d * 48 + l * 18 + (i % 3) * 6 + (j % 6)
                r = i - 3 if far_i else i + 3
                q = j - 6 if far_j else j + 6
                send[m, padded(lev, r, q)] = 1
                gather[tok, 192 + m] = 1
                send_out[m, tok] = 1
                place[padded(lev, r, q), 144 + m] = 1
    return [jnp.asarray(a, BF16) for a in (send, gather, send_out, place)]


def bias_kernel(table_ref, index_ref, bias_ref, tab, idx, idx_t, left):
    tab[...] = jnp.zeros_like(tab)
    tab[0:HEADS, 0:NBIAS] = table_ref[0, 0]
    idx[...] = jnp.zeros_like(idx)
    idx[:, 0:TOK] = index_ref[...]
    tail = idx[:, 128:256].astype(F32).T
    idx_t[:, 0:TOK] = tail[0:16].astype(jnp.int32)
    idx_t[:, TOK:256] = jnp.zeros((16, 256 - TOK), jnp.int32)
    left[...] = jnp.zeros_like(left)

    def look(flat, store):
        lo = flat & 127
        hi = flat >> 7
        for h in range(HEADS):
            acc = jnp.zeros((8, 128), F32)
            for t in range(NHI):
                row = jnp.broadcast_to(tab[h : h + 1, t * 128 : (t + 1) * 128], (8, 128))
                got = jnp.take_along_axis(row, lo, axis=1, mode="promise_in_bounds")
                acc = jnp.where(hi == t, got, acc)
            store(h, acc)

    def body(b, carry):
        at = pl.multiple_of(b * 8, 8)

        def store(h, acc):
            bias_ref[h, pl.ds(at, 8), 0:128] = acc

        look(idx[pl.ds(at, 8), 0:128], store)
        return carry

    lax.fori_loop(0, TOK // 8, body, 0)
    for a in range(2):
        for t in range(2):

            def store(h, acc, a=a, t=t):
                left[h, a * 8 : a * 8 + 8, t * 128 : (t + 1) * 128] = acc

            look(idx_t[a * 8 : a * 8 + 8, t * 128 : (t + 1) * 128], store)
    for h in range(HEADS):
        bias_ref[h, :, 128:TOK] = left[h].T[0:TOK, 0:16]


def layer_norm(values, gain_row, shift_row):
    centred = values - jnp.mean(values, -1, keepdims=True)
    inv_std = lax.rsqrt(jnp.mean(centred * centred, -1, keepdims=True) + NORM_EPS)
    normed = centred * inv_std
    return normed * gain_row + shift_row, normed, inv_std


def norm_back(incoming, normed, inv_std, gain_row):
    scaled = incoming * gain_row
    outgoing = inv_std * (
        scaled
        - jnp.mean(scaled, -1, keepdims=True)
        - normed * jnp.mean(scaled * normed, -1, keepdims=True)
    )
    return (
        outgoing,
        jnp.sum(incoming * normed, 0, keepdims=True),
        jnp.sum(incoming, 0, keepdims=True),
    )


def main_kernel(
    grid_ref,
    ids_ref,
    cot_ref,
    gain_ref,
    shift_ref,
    wqkv_ref,
    bqkv_ref,
    wproj_ref,
    bproj_ref,
    w1_ref,
    b1_ref,
    w2_ref,
    b2_ref,
    bias_ref,
    index_ref,
    send_sel,
    gather_sel,
    send_out_sel,
    place_sel,
    out_ref,
    din_ref,
    full_ref,
    tgrad_ref,
    stack,
    halo_msg,
    out_stack,
    out_msg,
    probs,
    act,
    dfac,
    dsc,
    small,
    grads,
    core_in1,
    core_in2,
    plane_in1,
    plane_in2,
    z_out,
    z_in,
    z_all,
    owned,
    t_out,
    t_in,
    halo_s,
    halo_r,
    oh_s,
    oh_r,
    core_s,
    core_r,
    plane_s,
    plane_r,
    zs,
    zr,
    zgs,
    zgr,
    ts,
    tr,
    tgs,
    tgr,
    ags,
    agr,
    fs,
    fr,
):
    lat = lax.axis_index("lat")
    lon = lax.axis_index("lon")
    core = lat % 2
    pair_lat = lat + 1 - 2 * core
    ylo = lon % 2
    z = lon // 2
    k = (lat // 2) * 2 + ylo
    lat_up, lat_dn = (lat + 1) % 16, (lat + 15) % 16
    lon_up, lon_dn = (lon + 1) % 32, (lon + 31) % 32

    def plane_device(kk):
        return ((kk // 2) * 2 + core, z * 2 + kk % 2)

    barrier = pltpu.get_barrier_semaphore()

    def greet(device):
        pl.semaphore_signal(barrier, inc=1, device_id=device, device_id_type=MESH)

    def greet_lon(d, carry):
        greet((lat, (lon + d) % 32))
        return carry

    def greet_plane(d, carry):
        greet(plane_device((k + d) % 16))
        return carry

    lax.fori_loop(1, 32, greet_lon, 0)
    lax.fori_loop(1, 16, greet_plane, 0)
    greet((pair_lat, lon))
    for device in ((lat_up, lon), (lat_dn, lon), (lat_up, lon_up), (lat_dn, lon_dn)):
        greet(device)

    stack[:, 0:192, :] = jnp.zeros((2, 192, 256), BF16)
    for l in range(2):
        for r in range(6):
            at = (l * 6 + r) * 16
            stack[0, at : at + 12, 0:C] = grid_ref[l, r]
            stack[1, at : at + 12, 0:C] = cot_ref[l, r]
            label = ids_ref[l, r : r + 1, 0:1].astype(F32)
            stack[0, at : at + 16, C:256] = jnp.broadcast_to(label, (16, 64)).astype(BF16)
    for n in range(2):
        halo_msg[n] = dot(send_sel[...], stack[n, 0:192, :]).astype(BF16)

    pl.semaphore_wait(barrier, 51)

    halo_to = ((lat, lon_dn), (lat_dn, lon), (lat_dn, lon_dn))
    halo = [
        pltpu.make_async_remote_copy(
            src_ref=halo_msg.at[:, d * 48 : (d + 1) * 48, :],
            dst_ref=stack.at[:, 192 + d * 48 : 192 + (d + 1) * 48, :],
            send_sem=halo_s.at[d],
            recv_sem=halo_r.at[d],
            device_id=halo_to[d],
            device_id_type=MESH,
        )
        for d in range(3)
    ]
    for copy in halo:
        copy.start()
    for copy in halo:
        copy.wait()

    win = dot(gather_sel[...], stack[0])
    g_b = dot(gather_sel[...], stack[1]).astype(BF16)[:, 0:C]
    x = win[:, 0:C]
    label_lane = win[:, 128:256].astype(BF16)
    pick = (lax.broadcasted_iota(jnp.int32, (8, 128), 1) == 64).astype(F32).astype(BF16)
    ids_row = dot(pick, label_lane, 1, 1)[0:1]
    ids_col = win[:, C : C + 1]
    allowed = ids_row == ids_col

    gain0, gain1 = gain_ref[0:1, :], gain_ref[1:2, :]
    shift0, shift1 = shift_ref[0:1, :], shift_ref[1:2, :]
    first, hat1, inv1 = layer_norm(x, gain0, shift0)
    first_b = first.astype(BF16)
    wq = wqkv_ref[:, 0:C]
    wk = wqkv_ref[:, C : 2 * C]
    wv = wqkv_ref[:, 2 * C : 3 * C]
    q = (dot(first_b, wq) + bqkv_ref[:, 0:C]).astype(BF16)
    key = (dot(first_b, wk) + bqkv_ref[:, C : 2 * C]).astype(BF16)
    v = (dot(first_b, wv) + bqkv_ref[:, 2 * C : 3 * C]).astype(BF16)
    lane = lax.broadcasted_iota(jnp.int32, (TOK, C), 1)

    def only(h, values):
        return jnp.where((lane >> 5) == h, values, jnp.zeros_like(values))

    mixed = jnp.zeros((TOK, C), F32)
    for h in range(HEADS):
        s = dot(only(h, q), key, 1, 1) * SCALE + bias_ref[h]
        s = jnp.where(allowed, s, NEG_FILL)
        e = jnp.exp(s - jnp.max(s, -1, keepdims=True))
        p = e * (1.0 / jnp.sum(e, -1, keepdims=True))
        probs[h] = p
        mixed = mixed + dot(p.astype(BF16), only(h, v))
    mixed_b = mixed.astype(BF16)
    attended = x + dot(mixed_b, wproj_ref[...]) + bproj_ref[...]

    second, hat2, inv2 = layer_norm(attended, gain1, shift1)
    second_b = second.astype(BF16)
    for b in range(FF // 128):
        cols = slice(b * 128, (b + 1) * 128)
        hidden = dot(second_b, w1_ref[:, cols]) + b1_ref[:, cols]
        cumul = 0.5 * (1.0 + lax.erf(hidden * ROOT_HALF))
        act[:, cols] = (hidden * cumul).astype(BF16)
        dfac[:, cols] = cumul + hidden * jnp.exp(-0.5 * hidden * hidden) * ROOT_TWOPI
    result = (attended + dot(act[...], w2_ref[...]) + b2_ref[...]).astype(BF16)

    halo_out_to = ((lat, lon_up), (lat_up, lon), (lat_up, lon_up))

    def send_back(n, values):
        out_stack[n, 0:TOK, 0:C] = values
        out_msg[n, :, 0:C] = dot(send_out_sel[...], values).astype(BF16)
        copies = [
            pltpu.make_async_remote_copy(
                src_ref=out_msg.at[n, d * 48 : (d + 1) * 48, :],
                dst_ref=out_stack.at[n, TOK + d * 48 : TOK + (d + 1) * 48, :],
                send_sem=oh_s.at[n, d],
                recv_sem=oh_r.at[n, d],
                device_id=halo_out_to[d],
                device_id_type=MESH,
            )
            for d in range(3)
        ]
        for copy in copies:
            copy.start()
        return copies

    out_copies = send_back(0, result)

    small[...] = jnp.zeros_like(small)

    def keep(row, vector):
        width = vector.shape[1]
        for at in range(0, width, 128):
            n = min(128, width - at)
            small[row + at // 128 : row + at // 128 + 1, 0:n] = vector[:, at : at + n]

    gf = g_b.astype(F32)
    keep(21, jnp.sum(gf, 0, keepdims=True))
    d_second = jnp.zeros((TOK, C), F32)
    for b in range(FF // 128):
        cols = slice(b * 128, (b + 1) * 128)
        grads[FC2_ROW + b * C : FC2_ROW + (b + 1) * C, :] = dot(g_b, act[:, cols], 0, 0).astype(BF16)
        d_hidden = dot(g_b, w2_ref[cols, :], 1, 1) * dfac[:, cols]
        d_hidden_b = d_hidden.astype(BF16)
        keep(15 + b, jnp.sum(d_hidden, 0, keepdims=True))
        grads[FC1_ROW + b * C : FC1_ROW + (b + 1) * C, :] = dot(second_b, d_hidden_b, 0, 0).astype(BF16)
        d_second = d_second + dot(d_hidden_b, w1_ref[:, cols], 1, 1)

    core_in = (core_in1, core_in2)
    plane_in = (plane_in1, plane_in2)

    def core_copy(n):
        base, rows = CHUNKS[n]
        return pltpu.make_async_remote_copy(
            src_ref=grads.at[pl.ds(pl.multiple_of(base + (1 - core) * 16 * rows, 16), 16 * rows), :],
            dst_ref=core_in[n],
            send_sem=core_s.at[n],
            recv_sem=core_r.at[n],
            device_id=(pair_lat, lon),
            device_id_type=MESH,
        )

    def add_core(n):
        base, rows = CHUNKS[n]
        mine = pl.ds(pl.multiple_of(base + core * 16 * rows, 16), 16 * rows)
        grads[mine, :] = (grads[mine, :].astype(F32) + core_in[n][...].astype(F32)).astype(BF16)

    def plane_copy(n, d):
        base, rows = CHUNKS[n]
        kk = (k + d) % 16
        return pltpu.make_async_remote_copy(
            src_ref=grads.at[pl.ds(pl.multiple_of(base + (core * 16 + kk) * rows, 16), rows), :],
            dst_ref=plane_in[n].at[d],
            send_sem=plane_s.at[n, d],
            recv_sem=plane_r.at[n, d],
            device_id=plane_device(kk),
            device_id_type=MESH,
        )

    def each(first_d, last_d, body):
        def step(d, carry):
            body(d)
            return carry

        lax.fori_loop(first_d, last_d, step, 0)

    def add_plane(n):
        base, rows = CHUNKS[n]
        total = grads[pl.ds(pl.multiple_of(base + (core * 16 + k) * rows, 16), rows), :].astype(F32)
        for d in range(1, 16):
            total = total + plane_in[n][d].astype(F32)
        return total

    core_copy(0).start()

    back2, dgain1, dshift1 = norm_back(d_second, hat2, inv2, gain1)
    keep(2, dgain1)
    keep(6, dshift1)
    d_att = gf + back2
    d_att_b = d_att.astype(BF16)
    core_copy(0).wait()
    add_core(0)
    each(1, 16, lambda d: plane_copy(0, d).start())

    def put_pair(at, left, right):
        grads[at : at + C, :] = left[:, 0:128].astype(BF16)
        grads[at + C : at + 2 * C, :] = right[:, 0:128].astype(BF16)
        grads[at + 2 * C : at + 3 * C, :] = jnp.concatenate([left[:, 128:C], right[:, 128:C]], 1).astype(BF16)

    dw_proj = dot(mixed_b, d_att_b, 0, 0)
    keep(13, jnp.sum(d_att, 0, keepdims=True))
    dm = dot(d_att_b, wproj_ref[...], 1, 1).astype(BF16)

    dq = jnp.zeros((TOK, C), F32)
    dk = jnp.zeros((TOK, C), F32)
    dv = jnp.zeros((TOK, C), F32)
    for h in range(HEADS):
        p = probs[h]
        dm_h = only(h, dm)
        dp = dot(dm_h, v, 1, 1)
        ds = p * (dp - jnp.sum(dp * p, -1, keepdims=True))
        dsc[h, :, 0:128] = ds[:, 0:128]
        dsc[h, :, 128:256] = jnp.concatenate([ds[:, 128:TOK], jnp.zeros((TOK, 112), F32)], 1)
        ds_b = (ds * SCALE).astype(BF16)
        dq = dq + dot(ds_b, only(h, key))
        dk = dk + dot(ds_b, only(h, q), 0, 0)
        dv = dv + dot(p.astype(BF16), dm_h, 0, 0)
    dq_b, dk_b, dv_b = dq.astype(BF16), dk.astype(BF16), dv.astype(BF16)
    put_pair(QP_ROW, dot(first_b, dq_b, 0, 0), dot(first_b, dk_b, 0, 0))
    put_pair(QP_ROW + 3 * C, dot(first_b, dv_b, 0, 0), dw_proj)
    d_bias = jnp.concatenate(
        [jnp.sum(dq, 0, keepdims=True), jnp.sum(dk, 0, keepdims=True), jnp.sum(dv, 0, keepdims=True)], 1
    )
    keep(8, d_bias)
    d_first = dot(dq_b, wq, 1, 1) + dot(dk_b, wk, 1, 1) + dot(dv_b, wv, 1, 1)
    back1, dgain0, dshift0 = norm_back(d_first, hat1, inv1, gain0)
    keep(0, dgain0)
    keep(4, dshift0)
    grads[SMALL_ROW : SMALL_ROW + 32, :] = small[...].astype(BF16)
    grads[SMALL_ROW + 32 : ROWS, :] = jnp.zeros((ROWS - SMALL_ROW - 32, 128), BF16)
    core_copy(1).start()
    din_copies = send_back(1, (d_att + back1).astype(BF16))
    core_copy(1).wait()
    add_core(1)
    each(1, 16, lambda d: plane_copy(1, d).start())

    hi_iota = lax.broadcasted_iota(jnp.int32, (32, 256), 0)
    lo_iota = lax.broadcasted_iota(jnp.int32, (128, 256), 0)

    def factors(flat, rows):
        width = flat.shape[1]
        is_hi = hi_iota[:, 0:width] == (flat >> 7)
        lo_hot = jnp.where(lo_iota[:, 0:width] == (flat & 127), 1.0, 0.0).astype(BF16)
        left = jnp.concatenate([jnp.where(is_hi, row, 0.0).astype(BF16) for row in rows], 0)
        return dot(left, lo_hot, 1, 1)

    def pairs(b, total):
        block = pl.ds(pl.multiple_of(b * 8, 8), 8)
        flat = index_ref[block, 0:128]
        rows = [dsc[h, block, 0:128] for h in range(HEADS)]
        two = lambda values, r: jnp.concatenate([values[r : r + 1], values[r + 1 : r + 2]], 1)
        for r in range(0, 8, 2):
            total = total + factors(two(flat, r), [two(values, r) for values in rows])
        return total

    table = lax.fori_loop(0, TOK // 8, pairs, jnp.zeros((HEADS * 32, 128), F32))
    flat_tail = jnp.concatenate([index_ref[:, 128:TOK].astype(F32), jnp.zeros((TOK, 112), F32)], 1).T[0:16]
    flat_tail = flat_tail.astype(jnp.int32)
    ds_tail = [dsc[h, :, 128:256].T for h in range(HEADS)]
    for r in range(16):
        table = table + factors(flat_tail[r : r + 1], [t[r : r + 1] for t in ds_tail])
    for n in range(32):
        t_out[n] = table[n * 6 : (n + 1) * 6]

    def t_copy(d):
        to = (lon + d) % 32
        return pltpu.make_async_remote_copy(
            src_ref=t_out.at[to],
            dst_ref=t_in.at[d],
            send_sem=ts.at[d],
            recv_sem=tr.at[d],
            device_id=(lat, to),
            device_id_type=MESH,
        )

    each(1, 32, lambda d: t_copy(d).start())

    each(1, 16, lambda d: plane_copy(0, d).wait())
    owned[0:64, :] = add_plane(0)
    each(1, 16, lambda d: plane_copy(1, d).wait())
    owned[64:OWNED, :] = add_plane(1)
    for n in range(16):
        z_out[n] = owned[n * ZROWS : (n + 1) * ZROWS, :]

    def z_copy(d):
        to = (z + d) % 16
        return pltpu.make_async_remote_copy(
            src_ref=z_out.at[to],
            dst_ref=z_in.at[d],
            send_sem=zs.at[d],
            recv_sem=zr.at[d],
            device_id=(lat, to * 2 + ylo),
            device_id_type=MESH,
        )

    def z_gather(d):
        to = (z + d) % 16
        return pltpu.make_async_remote_copy(
            src_ref=z_all.at[z],
            dst_ref=z_all.at[z],
            send_sem=zgs.at[d],
            recv_sem=zgr.at[d],
            device_id=(lat, to * 2 + ylo),
            device_id_type=MESH,
        )

    each(1, 16, lambda d: z_copy(d).start())
    each(1, 16, lambda d: z_copy(d).wait())
    total = z_out[z]
    for d in range(1, 16):
        total = total + z_in[d]
    z_all[z] = total
    each(1, 16, lambda d: z_gather(d).start())

    each(1, 32, lambda d: t_copy(d).wait())
    t_total = t_out[lon]
    for d in range(1, 32):
        t_total = t_total + t_in[d]
    tgrad_ref[lon] = t_total

    def t_gather(d):
        return pltpu.make_async_remote_copy(
            src_ref=tgrad_ref.at[lon],
            dst_ref=tgrad_ref.at[lon],
            send_sem=tgs.at[d],
            recv_sem=tgr.at[d],
            device_id=(lat, (lon + d) % 32),
            device_id_type=MESH,
        )

    each(1, 32, lambda d: t_gather(d).start())

    each(1, 16, lambda d: z_gather(d).wait())
    for n in range(16):
        owned[n * ZROWS : (n + 1) * ZROWS, :] = z_all[n]
    full_ref[core, k] = owned[...].astype(BF16)

    def plane_gather(d):
        return pltpu.make_async_remote_copy(
            src_ref=full_ref.at[core, k],
            dst_ref=full_ref.at[core, k],
            send_sem=ags.at[d],
            recv_sem=agr.at[d],
            device_id=plane_device((k + d) % 16),
            device_id_type=MESH,
        )

    def forward(d):
        kk = (k + 16 - d) % 16
        return pltpu.make_async_remote_copy(
            src_ref=full_ref.at[core, kk],
            dst_ref=full_ref.at[core, kk],
            send_sem=fs.at[d],
            recv_sem=fr.at[d],
            device_id=(pair_lat, lon),
            device_id_type=MESH,
        )

    each(1, 16, lambda d: plane_gather(d).start())
    forward(0).start()

    def pass_on(d):
        plane_gather(d).wait()
        forward(d).start()

    each(1, 16, pass_on)

    for n, copies, ref in ((0, out_copies, out_ref), (1, din_copies, din_ref)):
        for copy in copies:
            copy.wait()
        ref[...] = dot(place_sel[...], out_stack[n, :, 0:C]).astype(BF16)
    each(0, 16, lambda d: forward(d).wait())
    each(1, 32, lambda d: t_gather(d).wait())


def final_kernel(
    out_ref,
    din_ref,
    full_ref,
    tgrad_ref,
    output,
    grid_grad,
    gain_grad,
    shift_grad,
    dwqkv,
    dbqkv,
    dwproj,
    dbproj,
    dw1,
    db1,
    dw2,
    db2,
    dtable,
):
    for l in range(2):
        for r in range(6):
            at = (l * 6 + r) * 16
            output[l, r] = out_ref[at : at + 12, :]
            grid_grad[l, r] = din_ref[at : at + 12, :]

    def rows(start, count):
        parts = []
        at = start
        while at < start + count:
            n = 0 if at < CHUNKS[1][0] else 1
            base, size = CHUNKS[n]
            owner, inside = divmod(at - base, size)
            take = min(size - inside, start + count - at)
            first = inside + (0 if n == 0 else CHUNKS[0][1])
            parts.append(full_ref[owner // 16, owner % 16, first : first + take, :])
            at += take
        return jnp.concatenate(parts, 0).astype(F32) if len(parts) > 1 else parts[0].astype(F32)

    for b in range(FF // 128):
        cols = slice(b * 128, (b + 1) * 128)
        dw2[cols, :] = rows(FC2_ROW + b * C, C).T
        dw1[:, cols] = rows(FC1_ROW + b * C, C)
    qa, ka, qk = (rows(QP_ROW + n * C, C) for n in range(3))
    va, pa, vp = (rows(QP_ROW + n * C, C) for n in range(3, 6))
    dwqkv[:, 0:128] = qa
    dwqkv[:, 128:C] = qk[:, 0:64]
    dwqkv[:, C : C + 128] = ka
    dwqkv[:, C + 128 : 2 * C] = qk[:, 64:128]
    dwqkv[:, 2 * C : 2 * C + 128] = va
    dwqkv[:, 2 * C + 128 : 3 * C] = vp[:, 0:64]
    dwproj[:, 0:128] = pa
    dwproj[:, 128:C] = vp[:, 64:128]
    vec = rows(SMALL_ROW, 32)

    def load(row, width, ref, at=0):
        for n in range(0, width, 128):
            m = min(128, width - n)
            ref[at : at + 1, n : n + m] = vec[row + n // 128 : row + n // 128 + 1, 0:m]

    load(0, C, gain_grad, 0)
    load(2, C, gain_grad, 1)
    load(4, C, shift_grad, 0)
    load(6, C, shift_grad, 1)
    load(8, 3 * C, dbqkv)
    load(13, C, dbproj)
    load(15, FF, db1)
    load(21, C, db2)
    for h in range(HEADS):
        for t in range(NHI):
            n = h * 32 + t
            m = min(128, NBIAS - t * 128)
            dtable[0, 0, h : h + 1, t * 128 : t * 128 + m] = tgrad_ref[n // 6, n % 6 : n % 6 + 1, 0:m]


def on_device(
    grid,
    region_ids,
    cotangent,
    norm_gain,
    norm_shift,
    qkv_weight,
    qkv_bias,
    proj_weight,
    proj_bias,
    fc1_weight,
    fc1_bias,
    fc2_weight,
    fc2_bias,
    bias_table,
    pair_index,
):
    vmem = pl.BlockSpec(memory_space=pltpu.VMEM)
    shape = jax.ShapeDtypeStruct
    pair_bias = pl.pallas_call(
        bias_kernel,
        out_shape=shape((HEADS, TOK, TOK), F32),
        in_specs=[vmem] * 2,
        out_specs=vmem,
        scratch_shapes=[
            pltpu.VMEM((8, 3328), F32),
            pltpu.VMEM((TOK, 256), jnp.int32),
            pltpu.VMEM((16, 256), jnp.int32),
            pltpu.VMEM((HEADS, 128, 256), F32),
        ],
        name="pair_bias",
        compiler_params=pltpu.CompilerParams(vmem_limit_bytes=32 * 1024 * 1024),
    )(bias_table, pair_index)

    dma = pltpu.SemaphoreType.DMA
    out, din, full, tgrad = pl.pallas_call(
        main_kernel,
        out_shape=(
            shape((192, C), BF16),
            shape((192, C), BF16),
            shape((2, 16, OWNED, 128), BF16),
            shape((32, 6, 128), F32),
        ),
        in_specs=[vmem] * 19,
        out_specs=(vmem,) * 4,
        scratch_shapes=[
            pltpu.VMEM((2, 336, 256), BF16),
            pltpu.VMEM((2, 144, 256), BF16),
            pltpu.VMEM((2, 288, 256), BF16),
            pltpu.VMEM((2, 144, 256), BF16),
            pltpu.VMEM((HEADS, TOK, TOK), F32),
            pltpu.VMEM((TOK, FF), BF16),
            pltpu.VMEM((TOK, FF), F32),
            pltpu.VMEM((HEADS, TOK, 256), F32),
            pltpu.VMEM((32, 128), F32),
            pltpu.VMEM((ROWS, 128), BF16),
            pltpu.VMEM((1024, 128), BF16),
            pltpu.VMEM((768, 128), BF16),
            pltpu.VMEM((16, 64, 128), BF16),
            pltpu.VMEM((16, 48, 128), BF16),
            pltpu.VMEM((16, ZROWS, 128), F32),
            pltpu.VMEM((16, ZROWS, 128), F32),
            pltpu.VMEM((16, ZROWS, 128), F32),
            pltpu.VMEM((OWNED, 128), F32),
            pltpu.VMEM((32, 6, 128), F32),
            pltpu.VMEM((32, 6, 128), F32),
            dma((3,)),
            dma((3,)),
            dma((2, 3)),
            dma((2, 3)),
            dma((2,)),
            dma((2,)),
            dma((2, 16)),
            dma((2, 16)),
            dma((16,)),
            dma((16,)),
            dma((16,)),
            dma((16,)),
            dma((32,)),
            dma((32,)),
            dma((32,)),
            dma((32,)),
            dma((16,)),
            dma((16,)),
            dma((16,)),
            dma((16,)),
        ],
        name="window_block",
        compiler_params=pltpu.CompilerParams(
            collective_id=0, has_side_effects=True, vmem_limit_bytes=48 * 1024 * 1024
        ),
    )(
        grid,
        region_ids,
        cotangent,
        norm_gain,
        norm_shift,
        qkv_weight,
        qkv_bias[None],
        proj_weight,
        proj_bias[None],
        fc1_weight,
        fc1_bias[None],
        fc2_weight,
        fc2_bias[None],
        pair_bias,
        pair_index,
        *selectors(),
    )
    outs = pl.pallas_call(
        final_kernel,
        out_shape=(
            shape(grid.shape, BF16),
            shape(grid.shape, BF16),
            shape((2, C), F32),
            shape((2, C), F32),
            shape((C, 3 * C), F32),
            shape((1, 3 * C), F32),
            shape((C, C), F32),
            shape((1, C), F32),
            shape((C, FF), F32),
            shape((1, FF), F32),
            shape((FF, C), F32),
            shape((1, C), F32),
            shape(bias_table.shape, F32),
        ),
        in_specs=[vmem] * 4,
        out_specs=(vmem,) * 13,
        name="outputs",
        compiler_params=pltpu.CompilerParams(vmem_limit_bytes=32 * 1024 * 1024),
    )(out, din, full, tgrad)
    outs = list(outs)
    for n in (5, 7, 9, 11):
        outs[n] = outs[n][0]
    return tuple(outs)


def solution(mesh):
    field = P(None, "lat", "lon", None)
    table = P(None, "lat", None, None)
    return jax.shard_map(
        on_device,
        mesh=mesh,
        in_specs=(field, P(None, "lat", "lon"), field) + (P(),) * 10 + (table, P()),
        out_specs=(field, field) + (P(),) * 10 + (table,),
        check_vma=False,
    )
```

time: 860 us -> 86.4 us (0.10)
  waiting for transfers between devices: 363 us -> 0 us
  blocking collectives: 229 us -> 0 us
  other arithmetic: 123 us -> 1.21 us
  Pallas kernels: 0 us -> 75.9 us
  local copies, waits for them, and re-layouts: 75.9 us -> 8.13 us
  starting transfers between devices: 41.3 us -> 0 us
  between operations: 14.8 us -> 0.86 us
  matrix products: 10.9 us -> 0 us
    psum x1 -> x0, waiting for transfers between devices: 359 us -> none  [on_device(): lax.psum((gain_grad, shift_grad, att_grads[0], att_grads[1], att_grads[2]...]
    psum x2 -> x0, blocking collectives: 229 us -> none  [the longest x1 129 us: on_device(): lax.psum((gain_grad, shift_grad, att_grads[0], att_grads[1], att_grads[2]...]
    scatter-add x1 -> x0, other arithmetic: 113 us -> none  [table_gradient(): jax.ops.segment_sum(flat_terms.T, pair_index.reshape(-1), num_segments=NB...]
    pallas_call x0 -> x3, Pallas kernels: none -> 75.9 us  [the longest x1 69.3 us: on_device(): pl.pallas_call(main_kernel, out_shape=(shape((192, C), BF16), shape((192,...]
    gather x2 -> x0, local copies, waits for them, and re-layouts: 50.3 us -> none  [on_device(): pair_bias = jnp.take(bias_table, pair_index, axis=3)]
    ppermute x10 -> x0, starting transfers between devices: 41.3 us -> none  [passed_along(): return lax.ppermute(block, axis, route)]
    dot_general x18 -> x0, matrix products: 10.9 us -> none  [the longest x6 2.51 us: mixing(): jnp.einsum(form, left_op, right_op, preferred_element_type=jnp.float32)]
  transfers between devices with their start and end apart: 11 -> 0, of which waited for: 4 -> 0; matrix products, arithmetic and copies ran while one was open for 22% -> 0% of each run, Pallas kernels for 0% -> 0%
where the time goes in v1:
time: 86.4 us; the launch traced here: 86.1 us
  Pallas kernels  75.9 us (88%)
  local copies, waits for them, and re-layouts  8.13 us (9%)
  other arithmetic  1.21 us (1%)
    pallas_call x1, Pallas kernels, on_device(): pl.pallas_call(main_kernel, out_shape=(shape((192, C), BF16), shape((192,...  69.3 us
    unnamed x37, local copies, waits for them, and re-layouts  6.71 us
    pallas_call x1, Pallas kernels, on_device(): pl.pallas_call(bias_kernel, out_shape=shape((HEADS, TOK, TOK), F32), in_s...  5.32 us

profile of v1, /device:TPU:1, one launch (start us, length us, event | category | flops | bytes accessed | tf_op | source)
XLA Modules:
  0.0 86.1 jit_solution(17152143192576636907)
XLA Ops:
  0.6 0.0 copy-start.12
  0.7 0.7 broadcast_in_dim.12.bqkv_ref
  1.4 0.7 broadcast_in_dim.14.b1_ref
  2.1 0.7 copy.34.ids_ref
  2.8 0.9 %copy.33.grid_ref = bf16[2,6,12,192]{3,2,1,0:T(8,128)(2,1)S(1)} copy(bf16[2,6,12,192]{3,0,2,1:T(2,128)(2,1)} %param.19) | data formatting | bytes 110592 | tf_op args[0]
  3.7 0.0 copy-start.13
  3.7 0.9 %copy.35.cot_ref = bf16[2,6,12,192]{3,2,1,0:T(8,128)(2,1)S(1)} copy(bf16[2,6,12,192]{3,0,2,1:T(2,128)(2,1)} %param.21) | data formatting | bytes 110592 | tf_op args[2]
  4.6 0.0 copy-done.13
  4.7 0.0 copy-done.12
  4.7 0.0 copy-start
  4.7 0.2 copy.36.w2_ref
  4.8 0.7 copy-done
  5.6 0.0 copy-start.1
  5.6 0.0 copy-start.2
  5.6 0.0 copy-start.3
  5.6 0.0 copy-start.4
  5.6 0.0 copy-start.5
  5.6 0.0 copy-start.6
  5.6 0.0 copy-start.7
  5.6 0.0 copy-start.8
  5.6 0.0 copy-start.9
  5.6 0.0 copy-start.10
  5.7 0.0 copy-start.11
  5.7 5.3 %pair_bias.1.bias_ref = f32[6,144,144]{2,1,0:T(8,128)S(1)} custom-call(f32[1,1,6,3312]{3,2,1,0:T(8,128)S(1)} %copy.32.table_ref, s32[144,144]{1,0:T(8,128)S(1)} %copy-done), custom_call_target="tpu_custom_call" | custom-call | tf_op jit(solution)/shard_map/pair_bias/pallas_call | solution.py:676
  11.0 0.0 copy-done.1
  11.0 0.0 copy-done.2
  11.0 0.0 copy-done.3
  11.0 0.0 copy-done.4
  11.0 0.0 copy-done.5
  11.0 0.0 copy-done.6
  11.1 0.0 copy-done.7
  11.1 0.0 copy-done.8
  11.1 0.0 copy-done.9
  11.1 0.0 copy-done.10
  11.1 0.0 copy-done.11
  11.1 69.3 %window_block.1 = (bf16[192,192]{1,0:T(8,128)(2,1)S(1)}, bf16[192,192]{1,0:T(8,128)(2,1)S(1)}, bf16[2,16,112,128]{3,2,1,0:T(8,128)(2,1)S(1)}, f32[32,6,128]{2,1,0:T(8,128)S(1)}) custom-call(bf16[2,6,12,192]{3,2,1,0:T(8,128)(2,1)S(1)} %copy.33.grid_ref, s32[2,6,12]{2,1,0:T(8,128)S(1)} %copy.34.ids_ref, bf16[2,6,12,192]{3,2,1,0:T(8,128)(2,1)S(1)} %copy.35.cot_ref, ...), custom_call_target="tpu_custom_call" | custom-call | tf_op jit(solution)/shard_map/window_block/pallas_call | solution.py:692
  80.4 1.3 %outputs.1 = (bf16[2,6,12,192]{3,2,1,0:T(8,128)(2,1)S(1)}, bf16[2,6,12,192]{3,2,1,0:T(8,128)(2,1)S(1)}, f32[2,192]{1,0:T(2,128)}, f32[2,192]{1,0:T(2,128)}, f32[...) custom-call(bf16[192,192]{1,0:T(8,128)(2,1)S(1)} %get-tuple-element., ...), custom_call_target="tpu_custom_call" | custom-call | tf_op jit(solution)/shard_map/outputs/pallas_call | solution.py:766
  81.7 0.7 copy.37
  82.4 0.6 reduce
  83.0 0.6 reduce.1
  83.6 0.7 copy.38
  84.3 0.7 copy.40
  85.0 1.1 %copy.39 = f32[768,192]{0,1:T(8,128)} copy(f32[768,192]{1,0:T(8,128)S(1)} %get-tuple-element.57) | data formatting | bytes 1179648
  (1 shorter events, 0.0 us)
Async XLA Ops:
  0.6 4.0 %copy-start.12 = (bf16[768,192]{0,1:T(8,128)(2,1)S(1)}, bf16[768,192]{0,1:T(8,128)(2,1)}, u32[]{:S(2)}) copy-start(bf16[768,192]{0,1:T(8,128)(2,1)} %param.30) | copy-start | bytes 884740
  3.7 0.9 %copy-start.13 = (f32[1,1,6,3312]{3,1,2,0:T(1,128)S(1)}, f32[1,1,6,3312]{3,1,2,0:T(1,128)}, u32[]{:S(2)}) copy-start(f32[1,1,6,3312]{3,1,2,0:T(1,128)} %param.32) | copy-start | bytes 238468
  4.7 0.9 %copy-start = (s32[144,144]{1,0:T(8,128)S(1)}, s32[144,144]{1,0:T(8,128)}, u32[]{:S(2)}) copy-start(s32[144,144]{1,0:T(8,128)} %index_ref.3) | copy-start | bytes 248836
  5.6 5.4 %copy-start.1 = (bf16[192,768]{1,0:T(8,128)(2,1)S(1)}, bf16[192,768]{1,0:T(8,128)(2,1)}, u32[]{:S(2)}) copy-start(bf16[192,768]{1,0:T(8,128)(2,1)} %w1_ref.1) | copy-start | bytes 884740
  5.6 5.4 %copy-start.2 = (bf16[192,576]{1,0:T(8,128)(2,1)S(1)}, bf16[192,576]{1,0:T(8,128)(2,1)}, u32[]{:S(2)}) copy-start(bf16[192,576]{1,0:T(8,128)(2,1)} %wqkv_ref.1) | copy-start | bytes 663556
  5.6 5.4 %copy-start.3 = (bf16[192,288]{1,0:T(8,128)(2,1)S(1)}, bf16[192,288]{1,0:T(8,128)(2,1)}, u32[]{:S(2)}) copy-start(bf16[192,288]{1,0:T(8,128)(2,1)} %constant.11.clone.place_sel) | copy-start | bytes 331780
  5.6 5.4 %copy-start.4 = (bf16[144,336]{1,0:T(8,128)(2,1)S(1)}, bf16[144,336]{1,0:T(8,128)(2,1)}, u32[]{:S(2)}) copy-start(bf16[144,336]{1,0:T(8,128)(2,1)} %constant.9.clone.gather_sel) | copy-start | bytes 290308
  5.6 5.4 %copy-start.5 = (bf16[192,192]{1,0:T(8,128)(2,1)S(1)}, bf16[192,192]{1,0:T(8,128)(2,1)}, u32[]{:S(2)}) copy-start(bf16[192,192]{1,0:T(8,128)(2,1)} %wproj_ref.1) | copy-start | bytes 221188
  5.6 5.4 %copy-start.6 = (bf16[144,144]{1,0:T(8,128)(2,1)S(1)}, bf16[144,144]{1,0:T(8,128)(2,1)}, u32[]{:S(2)}) copy-start(bf16[144,144]{1,0:T(8,128)(2,1)} %constant.10.clone.send_out_sel) | copy-start | bytes 124420
  5.6 5.4 %copy-start.7 = (bf16[144,192]{1,0:T(8,128)(2,1)S(1)}, bf16[144,192]{1,0:T(8,128)(2,1)}, u32[]{:S(2)}) copy-start(bf16[144,192]{1,0:T(8,128)(2,1)} %constant.8.clone.send_sel) | copy-start | bytes 165892
  5.6 5.4 %copy-start.8 = (f32[2,192]{1,0:T(2,128)S(1)}, f32[2,192]{1,0:T(2,128)}, u32[]{:S(2)}) copy-start(f32[2,192]{1,0:T(2,128)} %gain_ref.1) | copy-start | bytes 4612
  5.6 5.4 %copy-start.9 = (f32[2,192]{1,0:T(2,128)S(1)}, f32[2,192]{1,0:T(2,128)}, u32[]{:S(2)}) copy-start(f32[2,192]{1,0:T(2,128)} %shift_ref.1) | copy-start | bytes 4612
  5.6 5.4 %copy-start.10 = (f32[192]{0:T(256)S(1)}, f32[192]{0:T(256)}, u32[]{:S(2)}) copy-start(f32[192]{0:T(256)} %param.27) | copy-start | bytes 2308
  5.7 5.4 %copy-start.11 = (f32[192]{0:T(256)S(1)}, f32[192]{0:T(256)}, u32[]{:S(2)}) copy-start(f32[192]{0:T(256)} %param.31) | copy-start | bytes 2308

commit v2 on v1

--- a/solution.py
+++ b/solution.py
@@ -40,35 +40,38 @@
 
 
 def selectors():
-    padded = lambda l, r, q: (l * 6 + r) * 16 + q
-    send = np.zeros((144, 192), np.float32)
-    gather = np.zeros((144, 336), np.float32)
+    held = lambda l, r, q: (r * 12 + q) * 2 + l
+    send = np.zeros((144, 144), np.float32)
+    gather = np.zeros((144, 288), np.float32)
     send_out = np.zeros((144, 144), np.float32)
-    place = np.zeros((192, 288), np.float32)
+    place = np.zeros((144, 288), np.float32)
+    label = np.zeros((144, 16), np.float32)
     for l in range(2):
         for i in range(6):
             for j in range(12):
+                label[held(l, i, j), i * 2 + l] = 1
                 tok = l * 72 + i * 12 + j
                 lev = (l + 1) % 2
                 far_i, far_j = i >= 3, j >= 6
+                r = i - 3 if far_i else i + 3
+                q = j - 6 if far_j else j + 6
                 if not far_i and not far_j:
-                    gather[tok, padded(lev, i + 3, j + 6)] = 1
-                    place[padded(lev, i + 3, j + 6), tok] = 1
+                    gather[tok, held(lev, r, q)] = 1
+                    place[held(lev, r, q), tok] = 1
                     continue
                 d = 2 if (far_i and far_j) else (1 if far_i else 0)
                 m = d * 48 + l * 18 + (i % 3) * 6 + (j % 6)
-                r = i - 3 if far_i else i + 3
-                q = j - 6 if far_j else j + 6
-                send[m, padded(lev, r, q)] = 1
-                gather[tok, 192 + m] = 1
+                send[m, held(lev, r, q)] = 1
+                gather[tok, 144 + m] = 1
                 send_out[m, tok] = 1
-                place[padded(lev, r, q), 144 + m] = 1
-    return [jnp.asarray(a, BF16) for a in (send, gather, send_out, place)]
-
-
-def bias_kernel(table_ref, index_ref, bias_ref, tab, idx, idx_t, left):
+                place[held(lev, r, q), 144 + m] = 1
+    return [jnp.asarray(a, BF16) for a in (send, gather, label, send_out, place)]
+
+
+def look_up_bias(table_ref, index_ref, bias_ref, tab, idx, idx_t, left):
     tab[...] = jnp.zeros_like(tab)
-    tab[0:HEADS, 0:NBIAS] = table_ref[0, 0]
+    for h in range(HEADS):
+        tab[h : h + 1, 0:NBIAS] = table_ref[0, h]
     idx[...] = jnp.zeros_like(idx)
     idx[:, 0:TOK] = index_ref[...]
     tail = idx[:, 128:256].astype(F32).T
@@ -106,6 +109,86 @@
             look(idx_t[a * 8 : a * 8 + 8, t * 128 : (t + 1) * 128], store)
     for h in range(HEADS):
         bias_ref[h, :, 128:TOK] = left[h].T[0:TOK, 0:16]
+
+
+def around():
+    lat = lax.axis_index("lat")
+    lon = lax.axis_index("lon")
+    return lat, lon, (lat + 1) % 16, (lat + 15) % 16, (lon + 1) % 32, (lon + 31) % 32
+
+
+def greet(device):
+    pl.semaphore_signal(pltpu.get_barrier_semaphore(), inc=1, device_id=device, device_id_type=MESH)
+
+
+def greet_halo():
+    lat, lon, lat_up, lat_dn, lon_up, lon_dn = around()
+    for device in (
+        (lat_up, lon),
+        (lat_dn, lon),
+        (lat, lon_up),
+        (lat, lon_dn),
+        (lat_up, lon_up),
+        (lat_dn, lon_dn),
+    ):
+        greet(device)
+
+
+def halo_kernel(
+    grid_ref,
+    ids_ref,
+    cot_ref,
+    table_ref,
+    index_ref,
+    send_sel,
+    gather_sel,
+    label_sel,
+    bias_ref,
+    win_ref,
+    stack,
+    halo_msg,
+    labels,
+    tab,
+    idx,
+    idx_t,
+    left,
+    halo_s,
+    halo_r,
+):
+    lat, lon, lat_up, lat_dn, lon_up, lon_dn = around()
+    greet_halo()
+    labels[...] = jnp.zeros_like(labels)
+    for r in range(6):
+        labels[2 * r : 2 * r + 2, :] = jnp.broadcast_to(ids_ref[r, :, 0:1].astype(F32), (2, 64))
+    stack[0, 0:TOK, C:256] = dot(label_sel[...], labels[...].astype(BF16)).astype(BF16)
+    stack[1, 0:TOK, C:256] = jnp.zeros((TOK, 64), BF16)
+    for r in range(6):
+        for q in range(12):
+            at = (r * 12 + q) * 2
+            stack[0, at : at + 2, 0:C] = grid_ref[r, q]
+            stack[1, at : at + 2, 0:C] = cot_ref[r, q]
+    for n in range(2):
+        halo_msg[n] = dot(send_sel[...], stack[n, 0:TOK, :]).astype(BF16)
+    pl.semaphore_wait(pltpu.get_barrier_semaphore(), 6)
+    halo_to = ((lat, lon_dn), (lat_dn, lon), (lat_dn, lon_dn))
+    halo = [
+        pltpu.make_async_remote_copy(
+            src_ref=halo_msg.at[:, d * 48 : (d + 1) * 48, :],
+            dst_ref=stack.at[:, TOK + d * 48 : TOK + (d + 1) * 48, :],
+            send_sem=halo_s.at[d],
+            recv_sem=halo_r.at[d],
+            device_id=halo_to[d],
+            device_id_type=MESH,
+        )
+        for d in range(3)
+    ]
+    for copy in halo:
+        copy.start()
+    look_up_bias(table_ref, index_ref, bias_ref, tab, idx, idx_t, left)
+    for copy in halo:
+        copy.wait()
+    for n in range(2):
+        win_ref[n] = dot(gather_sel[...], stack[n]).astype(BF16)
 
 
 def layer_norm(values, gain_row, shift_row):
@@ -130,9 +213,7 @@
 
 
 def main_kernel(
-    grid_ref,
-    ids_ref,
-    cot_ref,
+    win_ref,
     gain_ref,
     shift_ref,
     wqkv_ref,
@@ -145,16 +226,12 @@
     b2_ref,
     bias_ref,
     index_ref,
-    send_sel,
-    gather_sel,
     send_out_sel,
     place_sel,
     out_ref,
     din_ref,
     full_ref,
     tgrad_ref,
-    stack,
-    halo_msg,
     out_stack,
     out_msg,
     probs,
@@ -173,8 +250,6 @@
     owned,
     t_out,
     t_in,
-    halo_s,
-    halo_r,
     oh_s,
     oh_r,
     core_s,
@@ -194,87 +269,48 @@
     fs,
     fr,
 ):
-    lat = lax.axis_index("lat")
-    lon = lax.axis_index("lon")
+    lat, lon, lat_up, lat_dn, lon_up, lon_dn = around()
     core = lat % 2
     pair_lat = lat + 1 - 2 * core
     ylo = lon % 2
     z = lon // 2
     k = (lat // 2) * 2 + ylo
-    lat_up, lat_dn = (lat + 1) % 16, (lat + 15) % 16
-    lon_up, lon_dn = (lon + 1) % 32, (lon + 31) % 32
 
     def plane_device(kk):
         return ((kk // 2) * 2 + core, z * 2 + kk % 2)
 
-    barrier = pltpu.get_barrier_semaphore()
-
-    def greet(device):
-        pl.semaphore_signal(barrier, inc=1, device_id=device, device_id_type=MESH)
-
-    def greet_lon(d, carry):
-        greet((lat, (lon + d) % 32))
-        return carry
-
-    def greet_plane(d, carry):
-        greet(plane_device((k + d) % 16))
-        return carry
-
-    lax.fori_loop(1, 32, greet_lon, 0)
-    lax.fori_loop(1, 16, greet_plane, 0)
+    def each(first_d, last_d, body):
+        def step(d, carry):
+            body(d)
+            return carry
+
+        lax.fori_loop(first_d, last_d, step, 0)
+
+    each(1, 32, lambda d: greet((lat, (lon + d) % 32)))
+    each(1, 16, lambda d: greet(plane_device((k + d) % 16)))
     greet((pair_lat, lon))
-    for device in ((lat_up, lon), (lat_dn, lon), (lat_up, lon_up), (lat_dn, lon_dn)):
-        greet(device)
-
-    stack[:, 0:192, :] = jnp.zeros((2, 192, 256), BF16)
-    for l in range(2):
-        for r in range(6):
-            at = (l * 6 + r) * 16
-            stack[0, at : at + 12, 0:C] = grid_ref[l, r]
-            stack[1, at : at + 12, 0:C] = cot_ref[l, r]
-            label = ids_ref[l, r : r + 1, 0:1].astype(F32)
-            stack[0, at : at + 16, C:256] = jnp.broadcast_to(label, (16, 64)).astype(BF16)
-    for n in range(2):
-        halo_msg[n] = dot(send_sel[...], stack[n, 0:192, :]).astype(BF16)
-
-    pl.semaphore_wait(barrier, 51)
-
-    halo_to = ((lat, lon_dn), (lat_dn, lon), (lat_dn, lon_dn))
-    halo = [
-        pltpu.make_async_remote_copy(
-            src_ref=halo_msg.at[:, d * 48 : (d + 1) * 48, :],
-            dst_ref=stack.at[:, 192 + d * 48 : 192 + (d + 1) * 48, :],
-            send_sem=halo_s.at[d],
-            recv_sem=halo_r.at[d],
-            device_id=halo_to[d],
-            device_id_type=MESH,
-        )
-        for d in range(3)
-    ]
-    for copy in halo:
-        copy.start()
-    for copy in halo:
-        copy.wait()
-
-    win = dot(gather_sel[...], stack[0])
-    g_b = dot(gather_sel[...], stack[1]).astype(BF16)[:, 0:C]
-    x = win[:, 0:C]
-    label_lane = win[:, 128:256].astype(BF16)
+    greet_halo()
+
+    x = win_ref[0, :, 0:C].astype(F32)
+    g_b = win_ref[1, :, 0:C]
+    label_lane = win_ref[0, :, 128:256]
     pick = (lax.broadcasted_iota(jnp.int32, (8, 128), 1) == 64).astype(F32).astype(BF16)
     ids_row = dot(pick, label_lane, 1, 1)[0:1]
-    ids_col = win[:, C : C + 1]
+    ids_col = label_lane[:, 64:65].astype(F32)
     allowed = ids_row == ids_col
 
     gain0, gain1 = gain_ref[0:1, :], gain_ref[1:2, :]
     shift0, shift1 = shift_ref[0:1, :], shift_ref[1:2, :]
     first, hat1, inv1 = layer_norm(x, gain0, shift0)
     first_b = first.astype(BF16)
+    bqkv = bqkv_ref[...].reshape(1, 3 * C)
+    b1 = b1_ref[...].reshape(1, FF)
     wq = wqkv_ref[:, 0:C]
     wk = wqkv_ref[:, C : 2 * C]
     wv = wqkv_ref[:, 2 * C : 3 * C]
-    q = (dot(first_b, wq) + bqkv_ref[:, 0:C]).astype(BF16)
-    key = (dot(first_b, wk) + bqkv_ref[:, C : 2 * C]).astype(BF16)
-    v = (dot(first_b, wv) + bqkv_ref[:, 2 * C : 3 * C]).astype(BF16)
+    q = (dot(first_b, wq) + bqkv[:, 0:C]).astype(BF16)
+    key = (dot(first_b, wk) + bqkv[:, C : 2 * C]).astype(BF16)
+    v = (dot(first_b, wv) + bqkv[:, 2 * C : 3 * C]).astype(BF16)
     lane = lax.broadcasted_iota(jnp.int32, (TOK, C), 1)
 
     def only(h, values):
@@ -289,17 +325,17 @@
         probs[h] = p
         mixed = mixed + dot(p.astype(BF16), only(h, v))
     mixed_b = mixed.astype(BF16)
-    attended = x + dot(mixed_b, wproj_ref[...]) + bproj_ref[...]
+    attended = x + dot(mixed_b, wproj_ref[...]) + bproj_ref[...].reshape(1, C)
 
     second, hat2, inv2 = layer_norm(attended, gain1, shift1)
     second_b = second.astype(BF16)
     for b in range(FF // 128):
         cols = slice(b * 128, (b + 1) * 128)
-        hidden = dot(second_b, w1_ref[:, cols]) + b1_ref[:, cols]
+        hidden = dot(second_b, w1_ref[:, cols]) + b1[:, cols]
         cumul = 0.5 * (1.0 + lax.erf(hidden * ROOT_HALF))
         act[:, cols] = (hidden * cumul).astype(BF16)
         dfac[:, cols] = cumul + hidden * jnp.exp(-0.5 * hidden * hidden) * ROOT_TWOPI
-    result = (attended + dot(act[...], w2_ref[...]) + b2_ref[...]).astype(BF16)
+    result = (attended + dot(act[...], w2_ref[...], 1, 1) + b2_ref[...].reshape(1, C)).astype(BF16)
 
     halo_out_to = ((lat, lon_up), (lat_up, lon), (lat_up, lon_up))
 
@@ -321,8 +357,6 @@
             copy.start()
         return copies
 
-    out_copies = send_back(0, result)
-
     small[...] = jnp.zeros_like(small)
 
     def keep(row, vector):
@@ -337,7 +371,7 @@
     for b in range(FF // 128):
         cols = slice(b * 128, (b + 1) * 128)
         grads[FC2_ROW + b * C : FC2_ROW + (b + 1) * C, :] = dot(g_b, act[:, cols], 0, 0).astype(BF16)
-        d_hidden = dot(g_b, w2_ref[cols, :], 1, 1) * dfac[:, cols]
+        d_hidden = dot(g_b, w2_ref[:, cols]) * dfac[:, cols]
         d_hidden_b = d_hidden.astype(BF16)
         keep(15 + b, jnp.sum(d_hidden, 0, keepdims=True))
         grads[FC1_ROW + b * C : FC1_ROW + (b + 1) * C, :] = dot(second_b, d_hidden_b, 0, 0).astype(BF16)
@@ -374,13 +408,6 @@
             device_id_type=MESH,
         )
 
-    def each(first_d, last_d, body):
-        def step(d, carry):
-            body(d)
-            return carry
-
-        lax.fori_loop(first_d, last_d, step, 0)
-
     def add_plane(n):
         base, rows = CHUNKS[n]
         total = grads[pl.ds(pl.multiple_of(base + (core * 16 + k) * rows, 16), rows), :].astype(F32)
@@ -388,7 +415,9 @@
             total = total + plane_in[n][d].astype(F32)
         return total
 
+    pl.semaphore_wait(pltpu.get_barrier_semaphore(), 53)
     core_copy(0).start()
+    out_copies = send_back(0, result)
 
     back2, dgain1, dshift1 = norm_back(d_second, hat2, inv2, gain1)
     keep(2, dgain1)
@@ -599,11 +628,11 @@
     db2,
     dtable,
 ):
-    for l in range(2):
-        for r in range(6):
-            at = (l * 6 + r) * 16
-            output[l, r] = out_ref[at : at + 12, :]
-            grid_grad[l, r] = din_ref[at : at + 12, :]
+    for r in range(6):
+        for q in range(12):
+            at = (r * 12 + q) * 2
+            output[r, q] = out_ref[at : at + 2, :]
+            grid_grad[r, q] = din_ref[at : at + 2, :]
 
     def rows(start, count):
         parts = []
@@ -620,7 +649,7 @@
 
     for b in range(FF // 128):
         cols = slice(b * 128, (b + 1) * 128)
-        dw2[cols, :] = rows(FC2_ROW + b * C, C).T
+        dw2[:, cols] = rows(FC2_ROW + b * C, C)
         dw1[:, cols] = rows(FC1_ROW + b * C, C)
     qa, ka, qk = (rows(QP_ROW + n * C, C) for n in range(3))
     va, pa, vp = (rows(QP_ROW + n * C, C) for n in range(3, 6))
@@ -643,15 +672,16 @@
     load(2, C, gain_grad, 1)
     load(4, C, shift_grad, 0)
     load(6, C, shift_grad, 1)
-    load(8, 3 * C, dbqkv)
-    load(13, C, dbproj)
-    load(15, FF, db1)
-    load(21, C, db2)
+    for row, ref in ((8, dbqkv), (13, dbproj), (15, db1), (21, db2)):
+        width = ref.shape[0]
+        for n in range(0, width, 128):
+            m = min(128, width - n)
+            ref[n : n + m] = vec[row + n // 128, 0:m]
     for h in range(HEADS):
         for t in range(NHI):
             n = h * 32 + t
             m = min(128, NBIAS - t * 128)
-            dtable[0, 0, h : h + 1, t * 128 : t * 128 + m] = tgrad_ref[n // 6, n % 6 : n % 6 + 1, 0:m]
+            dtable[0, h, :, t * 128 : t * 128 + m] = tgrad_ref[n // 6, n % 6 : n % 6 + 1, 0:m]
 
 
 def on_device(
@@ -673,35 +703,50 @@
 ):
     vmem = pl.BlockSpec(memory_space=pltpu.VMEM)
     shape = jax.ShapeDtypeStruct
-    pair_bias = pl.pallas_call(
-        bias_kernel,
-        out_shape=shape((HEADS, TOK, TOK), F32),
-        in_specs=[vmem] * 2,
-        out_specs=vmem,
+    dma = pltpu.SemaphoreType.DMA
+    send_sel, gather_sel, label_sel, send_out_sel, place_sel = selectors()
+    by_tile = lambda field: field.transpose(1, 2, 0, 3)
+    bias, win = pl.pallas_call(
+        halo_kernel,
+        out_shape=(shape((HEADS, TOK, TOK), F32), shape((2, TOK, 256), BF16)),
+        in_specs=[vmem] * 8,
+        out_specs=(vmem,) * 2,
         scratch_shapes=[
+            pltpu.VMEM((2, 288, 256), BF16),
+            pltpu.VMEM((2, 144, 256), BF16),
+            pltpu.VMEM((16, 64), F32),
             pltpu.VMEM((8, 3328), F32),
             pltpu.VMEM((TOK, 256), jnp.int32),
             pltpu.VMEM((16, 256), jnp.int32),
             pltpu.VMEM((HEADS, 128, 256), F32),
+            dma((3,)),
+            dma((3,)),
         ],
-        name="pair_bias",
-        compiler_params=pltpu.CompilerParams(vmem_limit_bytes=32 * 1024 * 1024),
-    )(bias_table, pair_index)
-
-    dma = pltpu.SemaphoreType.DMA
+        name="halo_and_bias",
+        compiler_params=pltpu.CompilerParams(
+            collective_id=0, has_side_effects=True, vmem_limit_bytes=32 * 1024 * 1024
+        ),
+    )(
+        by_tile(grid),
+        region_ids.transpose(1, 0, 2),
+        by_tile(cotangent),
+        bias_table.transpose(0, 2, 1, 3),
+        pair_index,
+        send_sel,
+        gather_sel,
+        label_sel,
+    )
     out, din, full, tgrad = pl.pallas_call(
         main_kernel,
         out_shape=(
-            shape((192, C), BF16),
-            shape((192, C), BF16),
+            shape((TOK, C), BF16),
+            shape((TOK, C), BF16),
             shape((2, 16, OWNED, 128), BF16),
             shape((32, 6, 128), F32),
         ),
-        in_specs=[vmem] * 19,
+        in_specs=[vmem] * 15,
         out_specs=(vmem,) * 4,
         scratch_shapes=[
-            pltpu.VMEM((2, 336, 256), BF16),
-            pltpu.VMEM((2, 144, 256), BF16),
             pltpu.VMEM((2, 288, 256), BF16),
             pltpu.VMEM((2, 144, 256), BF16),
             pltpu.VMEM((HEADS, TOK, TOK), F32),
@@ -720,8 +765,6 @@
             pltpu.VMEM((OWNED, 128), F32),
             pltpu.VMEM((32, 6, 128), F32),
             pltpu.VMEM((32, 6, 128), F32),
-            dma((3,)),
-            dma((3,)),
             dma((2, 3)),
             dma((2, 3)),
             dma((2,)),
@@ -743,42 +786,41 @@
         ],
         name="window_block",
         compiler_params=pltpu.CompilerParams(
-            collective_id=0, has_side_effects=True, vmem_limit_bytes=48 * 1024 * 1024
+            collective_id=1, has_side_effects=True, vmem_limit_bytes=48 * 1024 * 1024
         ),
     )(
-        grid,
-        region_ids,
-        cotangent,
+        win,
         norm_gain,
         norm_shift,
         qkv_weight,
-        qkv_bias[None],
+        qkv_bias,
         proj_weight,
-        proj_bias[None],
+        proj_bias,
         fc1_weight,
-        fc1_bias[None],
-        fc2_weight,
-        fc2_bias[None],
-        pair_bias,
+        fc1_bias,
+        fc2_weight.T,
+        fc2_bias,
+        bias,
         pair_index,
-        *selectors(),
+        send_out_sel,
+        place_sel,
     )
     outs = pl.pallas_call(
         final_kernel,
         out_shape=(
-            shape(grid.shape, BF16),
-            shape(grid.shape, BF16),
+            shape((6, 12, 2, C), BF16),
+            shape((6, 12, 2, C), BF16),
             shape((2, C), F32),
             shape((2, C), F32),
             shape((C, 3 * C), F32),
-            shape((1, 3 * C), F32),
+            shape((3 * C,), F32),
             shape((C, C), F32),
-            shape((1, C), F32),
+            shape((C,), F32),
             shape((C, FF), F32),
-            shape((1, FF), F32),
-            shape((FF, C), F32),
-            shape((1, C), F32),
-            shape(bias_table.shape, F32),
+            shape((FF,), F32),
+            shape((C, FF), F32),
+            shape((C,), F32),
+            shape((1, HEADS, 1, NBIAS), F32),
         ),
         in_specs=[vmem] * 4,
         out_specs=(vmem,) * 13,
@@ -786,8 +828,10 @@
         compiler_params=pltpu.CompilerParams(vmem_limit_bytes=32 * 1024 * 1024),
     )(out, din, full, tgrad)
     outs = list(outs)
-    for n in (5, 7, 9, 11):
-        outs[n] = outs[n][0]
+    for n in (0, 1):
+        outs[n] = outs[n].transpose(2, 0, 1, 3)
+    outs[10] = outs[10].T
+    outs[12] = outs[12].transpose(0, 2, 1, 3)
     return tuple(outs)
 
 

time: 86.4 us -> 84.5 us (0.978)
  Pallas kernels: 75.9 us -> 71.9 us
  local copies, waits for them, and re-layouts: 8.13 us -> 11.1 us
  other arithmetic: 1.21 us -> 0 us
    unnamed x37 -> x42, local copies, waits for them, and re-layouts: 6.71 us -> 11.1 us
    pallas_call x3, Pallas kernels: 75.9 us -> 71.9 us  [the longest x1 52.3 us: on_device(): pl.pallas_call(main_kernel, out_shape=(shape((TOK, C), BF16), shape((TOK,...]
    broadcast_in_dim x2 -> x0, local copies, waits for them, and re-layouts: 1.42 us -> none  [the longest x1 0.73 us: on_device(): qkv_bias[None]]
    pallas_call x2 -> x0, other arithmetic: 1.21 us -> none  [on_device(): pl.pallas_call(final_kernel, out_shape=(shape(grid.shape, BF16), shape(gr...]
where the time goes in v2:
time: 84.5 us; the launch traced here: 83.8 us
  Pallas kernels  71.9 us (85%)
  local copies, waits for them, and re-layouts  11.1 us (13%)
    pallas_call x1, Pallas kernels, on_device(): pl.pallas_call(main_kernel, out_shape=(shape((TOK, C), BF16), shape((TOK,...  52.3 us
    pallas_call x1, Pallas kernels, on_device(): pl.pallas_call(halo_kernel, out_shape=(shape((HEADS, TOK, TOK), F32), sha...  18.2 us
    unnamed x42, local copies, waits for them, and re-layouts  11.1 us

profile of v2, /device:TPU:1, one launch (start us, length us, event | category | flops | bytes accessed | tf_op | source)
XLA Modules:
  0.0 83.8 jit_solution(4997526271236945341)
XLA Ops:
  0.6 0.0 copy-start.14
  0.7 0.7 copy-done.14
  1.3 0.0 copy-start
  1.3 0.9 %copy-done = s32[144,144]{1,0:T(8,128)S(1)} copy-done((s32[144,144]{1,0:T(8,128)S(1)}, s32[144,144]{1,0:T(8,128)}, u32[]{:S(2)}) %copy-start) | copy-done | bytes 82968
  2.3 0.0 copy-start.5
  2.3 0.9 %copy-done.5 = bf16[144,288]{1,0:T(8,128)(2,1)S(1)} copy-done((bf16[144,288]{1,0:T(8,128)(2,1)S(1)}, bf16[144,288]{1,0:T(8,128)(2,1)}, u32[]{:S(2)}) %copy-start.5) | copy-done | bytes 82968
  3.1 0.0 copy-start.8
  3.2 0.9 %copy-done.8 = f32[1,1,6,3312]{3,1,2,0:T(1,128)S(1)} copy-done((f32[1,1,6,3312]{3,1,2,0:T(1,128)S(1)}, f32[1,1,6,3312]{3,1,2,0:T(1,128)}, u32[]{:S(2)}) %copy-start.8) | copy-done | bytes 79512
  4.0 0.0 copy-start.9
  4.0 0.9 %copy-done.9 = bf16[2,6,12,192]{3,0,2,1:T(2,128)(2,1)S(1)} copy-done((bf16[2,6,12,192]{3,0,2,1:T(2,128)(2,1)S(1)}, bf16[2,6,12,192]{3,0,2,1:T(2,128)(2,1)}, u32[]{:S(2)}) %copy-start.9) | copy-done | bytes 55320
  4.9 0.0 copy-start.10
  4.9 0.9 %copy-done.10 = bf16[2,6,12,192]{3,0,2,1:T(2,128)(2,1)S(1)} copy-done((bf16[2,6,12,192]{3,0,2,1:T(2,128)(2,1)S(1)}, bf16[2,6,12,192]{3,0,2,1:T(2,128)(2,1)}, u32[]{:S(2)}) %copy-start.10) | copy-done | bytes 55320
  5.8 0.0 copy-start.11
  5.8 0.9 %copy-done.11 = bf16[144,144]{1,0:T(8,128)(2,1)S(1)} copy-done((bf16[144,144]{1,0:T(8,128)(2,1)S(1)}, bf16[144,144]{1,0:T(8,128)(2,1)}, u32[]{:S(2)}) %copy-start.11) | copy-done | bytes 41496
  6.7 0.0 copy-start.13
  6.7 0.8 copy-done.13
  7.5 0.0 copy-start.1
  7.5 0.0 copy-start.2
  7.5 0.0 copy-start.6
  7.5 0.0 copy-start.15
  7.5 0.0 copy-start.16
  7.5 0.0 copy-start.18
  7.5 0.0 copy-start.20
  7.5 18.2 %halo_and_bias.1 = (f32[6,144,144]{2,1,0:T(8,128)S(1)}, bf16[2,144,256]{2,1,0:T(8,128)(2,1)S(1)}) custom-call(bf16[6,12,2,192]{3,2,1,0:T(2,128)(2,1)S(1)} %bitcast.13, s32[6,2,12]{2,1,0:T(2,128)S(1)} %bitcast.15, bf16[6,12,2,192]{3,2,1,0:T(2,128)(2,1)S(1)} %bitcast.14, f32[1,6,1,3312]{3,2,1,0:T(1,128)S(1)} %bitcast.12, s32[144,144]{1,0:T(8,128)S(1)} %copy-done, ...), custom_call_target="tpu_custom_call" | custom-call | tf_op jit(solution)/shard_map/halo_and_bias/pallas_call | solution.py:709
  25.7 0.0 copy-start.17
  25.7 0.0 copy-start.19
  25.7 0.0 copy-done.1
  25.8 0.0 copy-done.2
  25.8 0.0 copy-done.6
  25.8 0.0 copy-done.15
  25.8 0.0 copy-done.16
  25.8 0.0 copy-done.18
  25.8 0.0 copy-done.20
  25.8 0.6 copy-done.17
  26.4 0.0 copy-done.19
  26.4 0.0 copy-start.3
  26.4 1.0 %copy-done.3 = bf16[768,192]{0,1:T(8,128)(2,1)S(1)} copy-done((bf16[768,192]{0,1:T(8,128)(2,1)S(1)}, bf16[768,192]{0,1:T(8,128)(2,1)}, u32[]{:S(2)}) %copy-start.3) | copy-done | bytes 294936
  27.4 0.0 copy-start.4
  27.4 0.9 %copy-done.4 = bf16[192,576]{1,0:T(8,128)(2,1)S(1)} copy-done((bf16[192,576]{1,0:T(8,128)(2,1)S(1)}, bf16[192,576]{1,0:T(8,128)(2,1)}, u32[]{:S(2)}) %copy-start.4) | copy-done | bytes 221208
  28.3 0.0 copy-start.7
  28.3 0.9 %copy-done.7 = bf16[192,192]{1,0:T(8,128)(2,1)S(1)} copy-done((bf16[192,192]{1,0:T(8,128)(2,1)S(1)}, bf16[192,192]{1,0:T(8,128)(2,1)}, u32[]{:S(2)}) %copy-start.7) | copy-done | bytes 73752
  29.2 0.0 copy-start.12
  29.2 0.9 %copy-done.12 = bf16[144,144]{1,0:T(8,128)(2,1)S(1)} copy-done((bf16[144,144]{1,0:T(8,128)(2,1)S(1)}, bf16[144,144]{1,0:T(8,128)(2,1)}, u32[]{:S(2)}) %copy-start.12) | copy-done | bytes 41496
  30.1 52.3 %window_block.1 = (bf16[144,192]{1,0:T(8,128)(2,1)S(1)}, bf16[144,192]{1,0:T(8,128)(2,1)S(1)}, bf16[2,16,112,128]{3,2,1,0:T(8,128)(2,1)S(1)}, f32[32,6,128]{2,1,0:T(8,128)S(1)}) custom-call(bf16[2,144,256]{2,1,0:T(8,128)(2,1)S(1)} %get-tuple-element.32.win_ref, f32[2,192]{1,0:T(2,128)S(1)} %copy-done.17, f32[2,192]{1,0:T(2,128)S(1)} %copy-done.18, ...), custom_call_target="tpu_custom_call" | custom-call | tf_op jit(solution)/shard_map/window_block/pallas_call | solution.py:739
  82.4 1.4 %outputs.1 = (bf16[6,12,2,192]{3,2,1,0:T(2,128)(2,1)}, bf16[6,12,2,192]{3,2,1,0:T(2,128)(2,1)}, f32[2,192]{1,0:T(2,128)}, f32[2,192]{1,0:T(2,128)}, f32[192,576]...) custom-call(bf16[144,192]{1,0:T(8,128)(2,1)S(1)} %get-tuple-element., ...), custom_call_target="tpu_custom_call" | custom-call | tf_op jit(solution)/shard_map/outputs/pallas_call | solution.py:808
Async XLA Ops:
  0.6 0.7 copy-start.14
  1.3 0.9 %copy-start = (s32[144,144]{1,0:T(8,128)S(1)}, s32[144,144]{1,0:T(8,128)}, u32[]{:S(2)}) copy-start(s32[144,144]{1,0:T(8,128)} %index_ref.3) | copy-start | bytes 248836
  2.3 0.9 %copy-start.5 = (bf16[144,288]{1,0:T(8,128)(2,1)S(1)}, bf16[144,288]{1,0:T(8,128)(2,1)}, u32[]{:S(2)}) copy-start(bf16[144,288]{1,0:T(8,128)(2,1)} %constant.11.clone.gather_sel) | copy-start | bytes 248836
  3.1 0.9 %copy-start.8 = (f32[1,1,6,3312]{3,1,2,0:T(1,128)S(1)}, f32[1,1,6,3312]{3,1,2,0:T(1,128)}, u32[]{:S(2)}) copy-start(f32[1,1,6,3312]{3,1,2,0:T(1,128)} %param.33) | copy-start | bytes 238468
  4.0 0.9 %copy-start.9 = (bf16[2,6,12,192]{3,0,2,1:T(2,128)(2,1)S(1)}, bf16[2,6,12,192]{3,0,2,1:T(2,128)(2,1)}, u32[]{:S(2)}) copy-start(bf16[2,6,12,192]{3,0,2,1:T(2,128)(2,1)} %param.20) | copy-start | bytes 165892
  4.9 0.9 %copy-start.10 = (bf16[2,6,12,192]{3,0,2,1:T(2,128)(2,1)S(1)}, bf16[2,6,12,192]{3,0,2,1:T(2,128)(2,1)}, u32[]{:S(2)}) copy-start(bf16[2,6,12,192]{3,0,2,1:T(2,128)(2,1)} %param.22) | copy-start | bytes 165892
  5.8 0.9 %copy-start.11 = (bf16[144,144]{1,0:T(8,128)(2,1)S(1)}, bf16[144,144]{1,0:T(8,128)(2,1)}, u32[]{:S(2)}) copy-start(bf16[144,144]{1,0:T(8,128)(2,1)} %constant.10.clone.send_sel) | copy-start | bytes 124420
  6.7 0.8 copy-start.13
  7.5 18.3 %copy-start.1 = (s32[144,144]{1,0:T(8,128)S(1)}, s32[144,144]{1,0:T(8,128)}, u32[]{:S(2)}) copy-start(s32[144,144]{1,0:T(8,128)} %index_ref.3) | copy-start | bytes 248836
  7.5 18.3 %copy-start.2 = (bf16[192,768]{1,0:T(8,128)(2,1)S(1)}, bf16[192,768]{1,0:T(8,128)(2,1)}, u32[]{:S(2)}) copy-start(bf16[192,768]{1,0:T(8,128)(2,1)} %w1_ref.1) | copy-start | bytes 884740
  7.5 18.3 %copy-start.6 = (bf16[144,288]{1,0:T(8,128)(2,1)S(1)}, bf16[144,288]{1,0:T(8,128)(2,1)}, u32[]{:S(2)}) copy-start(bf16[144,288]{1,0:T(8,128)(2,1)} %constant.14.clone.place_sel) | copy-start | bytes 248836
  7.5 18.3 %copy-start.15 = (f32[576]{0:T(1024)S(1)}, f32[576]{0:T(1024)}, u32[]{:S(2)}) copy-start(f32[576]{0:T(1024)} %bqkv_ref.1) | copy-start | bytes 6916
  7.5 18.3 %copy-start.16 = (f32[768]{0:T(1024)S(1)}, f32[768]{0:T(1024)}, u32[]{:S(2)}) copy-start(f32[768]{0:T(1024)} %b1_ref.1) | copy-start | bytes 9220
  7.5 18.3 %copy-start.18 = (f32[2,192]{1,0:T(2,128)S(1)}, f32[2,192]{1,0:T(2,128)}, u32[]{:S(2)}) copy-start(f32[2,192]{1,0:T(2,128)} %shift_ref.1) | copy-start | bytes 4612
  7.5 18.3 %copy-start.20 = (f32[192]{0:T(256)S(1)}, f32[192]{0:T(256)}, u32[]{:S(2)}) copy-start(f32[192]{0:T(256)} %b2_ref.1) | copy-start | bytes 2308
  25.7 0.7 copy-start.17
  25.7 0.7 copy-start.19
  26.4 1.0 %copy-start.3 = (bf16[768,192]{0,1:T(8,128)(2,1)S(1)}, bf16[768,192]{0,1:T(8,128)(2,1)}, u32[]{:S(2)}) copy-start(bf16[768,192]{0,1:T(8,128)(2,1)} %param.31) | copy-start | bytes 884740
  27.4 0.9 %copy-start.4 = (bf16[192,576]{1,0:T(8,128)(2,1)S(1)}, bf16[192,576]{1,0:T(8,128)(2,1)}, u32[]{:S(2)}) copy-start(bf16[192,576]{1,0:T(8,128)(2,1)} %wqkv_ref.1) | copy-start | bytes 663556
  28.3 0.9 %copy-start.7 = (bf16[192,192]{1,0:T(8,128)(2,1)S(1)}, bf16[192,192]{1,0:T(8,128)(2,1)}, u32[]{:S(2)}) copy-start(bf16[192,192]{1,0:T(8,128)(2,1)} %wproj_ref.1) | copy-start | bytes 221188
  29.2 0.9 %copy-start.12 = (bf16[144,144]{1,0:T(8,128)(2,1)S(1)}, bf16[144,144]{1,0:T(8,128)(2,1)}, u32[]{:S(2)}) copy-start(bf16[144,144]{1,0:T(8,128)(2,1)} %constant.13.clone.send_out_sel) | copy-start | bytes 124420

commit v3 on v2

--- a/solution.py
+++ b/solution.py
@@ -32,7 +32,7 @@
 SMALL_ROW = 3456
 CHUNKS = ((0, 64), (2048, 48))
 OWNED = 112
-ZROWS = 7
+PASSED = 12
 
 
 def dot(a, b, ca=1, cb=0):
@@ -134,29 +134,54 @@
         greet(device)
 
 
-def halo_kernel(
-    grid_ref,
-    ids_ref,
-    cot_ref,
-    table_ref,
-    index_ref,
-    send_sel,
-    gather_sel,
-    label_sel,
-    bias_ref,
-    win_ref,
-    stack,
-    halo_msg,
-    labels,
-    tab,
-    idx,
-    idx_t,
-    left,
-    halo_s,
-    halo_r,
-):
+def halo_kernel(*refs):
+    grid_hbm, cot_hbm, ids_hbm, send_hbm, label_hbm, table_hbm, index_hbm, gather_hbm = refs[0:8]
+    weights_hbm = refs[8 : 8 + PASSED]
+    bias_ref, win_ref, index_ref = refs[8 + PASSED : 11 + PASSED]
+    weights_ref = refs[11 + PASSED : 11 + 2 * PASSED]
+    (
+        grid_ref,
+        cot_ref,
+        ids_ref,
+        send_sel,
+        label_sel,
+        table_ref,
+        gather_sel,
+        stack,
+        halo_msg,
+        labels,
+        tab,
+        idx,
+        idx_t,
+        left,
+        halo_s,
+        halo_r,
+        load_s,
+    ) = refs[11 + 2 * PASSED :]
+    loads = [
+        pltpu.make_async_copy(src, dst, load_s.at[n])
+        for n, (src, dst) in enumerate(
+            (
+                (grid_hbm, grid_ref),
+                (cot_hbm, cot_ref),
+                (ids_hbm, ids_ref),
+                (send_hbm, send_sel),
+                (label_hbm, label_sel),
+                (table_hbm, table_ref),
+                (index_hbm, index_ref),
+                (gather_hbm, gather_sel),
+                *zip(weights_hbm, weights_ref),
+            )
+        )
+    ]
+    for load in loads[0:8]:
+        load.start()
     lat, lon, lat_up, lat_dn, lon_up, lon_dn = around()
     greet_halo()
+    for load in loads[8:]:
+        load.start()
+    for load in loads[0:5]:
+        load.wait()
     labels[...] = jnp.zeros_like(labels)
     for r in range(6):
         labels[2 * r : 2 * r + 2, :] = jnp.broadcast_to(ids_ref[r, :, 0:1].astype(F32), (2, 64))
@@ -184,7 +209,11 @@
     ]
     for copy in halo:
         copy.start()
+    for load in loads[5:8]:
+        load.wait()
     look_up_bias(table_ref, index_ref, bias_ref, tab, idx, idx_t, left)
+    for load in loads[8:]:
+        load.wait()
     for copy in halo:
         copy.wait()
     for n in range(2):
@@ -377,6 +406,7 @@
         grads[FC1_ROW + b * C : FC1_ROW + (b + 1) * C, :] = dot(second_b, d_hidden_b, 0, 0).astype(BF16)
         d_second = d_second + dot(d_hidden_b, w1_ref[:, cols], 1, 1)
 
+    z_out[...] = jnp.zeros_like(z_out)
     core_in = (core_in1, core_in2)
     plane_in = (plane_in1, plane_in2)
 
@@ -390,11 +420,6 @@
             device_id=(pair_lat, lon),
             device_id_type=MESH,
         )
-
-    def add_core(n):
-        base, rows = CHUNKS[n]
-        mine = pl.ds(pl.multiple_of(base + core * 16 * rows, 16), 16 * rows)
-        grads[mine, :] = (grads[mine, :].astype(F32) + core_in[n][...].astype(F32)).astype(BF16)
 
     def plane_copy(n, d):
         base, rows = CHUNKS[n]
@@ -408,12 +433,93 @@
             device_id_type=MESH,
         )
 
-    def add_plane(n):
+    def z_copy(n, d):
+        to = (z + d) % 16
+        return pltpu.make_async_remote_copy(
+            src_ref=z_out.at[n, to],
+            dst_ref=z_in.at[n, d],
+            send_sem=zs.at[n, d],
+            recv_sem=zr.at[n, d],
+            device_id=(lat, to * 2 + ylo),
+            device_id_type=MESH,
+        )
+
+    def z_gather(n, d):
+        to = (z + d) % 16
+        return pltpu.make_async_remote_copy(
+            src_ref=z_all.at[n, z],
+            dst_ref=z_all.at[n, z],
+            send_sem=zgs.at[n, d],
+            recv_sem=zgr.at[n, d],
+            device_id=(lat, to * 2 + ylo),
+            device_id_type=MESH,
+        )
+
+    def owner_rows(n):
+        return slice(0, 64) if n == 0 else slice(64, OWNED)
+
+    def plane_gather(n, d):
+        return pltpu.make_async_remote_copy(
+            src_ref=full_ref.at[core, k, owner_rows(n)],
+            dst_ref=full_ref.at[core, k, owner_rows(n)],
+            send_sem=ags.at[n, d],
+            recv_sem=agr.at[n, d],
+            device_id=plane_device((k + d) % 16),
+            device_id_type=MESH,
+        )
+
+    def forward(n, d):
+        kk = (k + 16 - d) % 16
+        return pltpu.make_async_remote_copy(
+            src_ref=full_ref.at[core, kk, owner_rows(n)],
+            dst_ref=full_ref.at[core, kk, owner_rows(n)],
+            send_sem=fs.at[n, d],
+            recv_sem=fr.at[n, d],
+            device_id=(pair_lat, lon),
+            device_id_type=MESH,
+        )
+
+    def scatter_plane(n):
         base, rows = CHUNKS[n]
+        core_copy(n).wait()
+        mine = pl.ds(pl.multiple_of(base + core * 16 * rows, 16), 16 * rows)
+        grads[mine, :] = (grads[mine, :].astype(F32) + core_in[n][...].astype(F32)).astype(BF16)
+        each(1, 16, lambda d: plane_copy(n, d).start())
+
+    def scatter_z(n):
+        base, rows = CHUNKS[n]
+        per = rows // 16
+        each(1, 16, lambda d: plane_copy(n, d).wait())
         total = grads[pl.ds(pl.multiple_of(base + (core * 16 + k) * rows, 16), rows), :].astype(F32)
         for d in range(1, 16):
             total = total + plane_in[n][d].astype(F32)
-        return total
+        for m in range(16):
+            z_out[n, m, 0:per] = total[m * per : (m + 1) * per]
+        each(1, 16, lambda d: z_copy(n, d).start())
+
+    def gather_z(n):
+        each(1, 16, lambda d: z_copy(n, d).wait())
+        total = z_out[n, z]
+        for d in range(1, 16):
+            total = total + z_in[n, d]
+        z_all[n, z] = total
+        each(1, 16, lambda d: z_gather(n, d).start())
+
+    def gather_plane(n):
+        per = CHUNKS[n][1] // 16
+        each(1, 16, lambda d: z_gather(n, d).wait())
+        for m in range(16):
+            owned[m * per : (m + 1) * per, :] = z_all[n, m, 0:per]
+        full_ref[core, k, owner_rows(n)] = owned[0 : CHUNKS[n][1], :].astype(BF16)
+        each(1, 16, lambda d: plane_gather(n, d).start())
+        forward(n, 0).start()
+
+    def pass_on(n):
+        def step(d):
+            plane_gather(n, d).wait()
+            forward(n, d).start()
+
+        each(1, 16, step)
 
     pl.semaphore_wait(pltpu.get_barrier_semaphore(), 53)
     core_copy(0).start()
@@ -424,9 +530,7 @@
     keep(6, dshift1)
     d_att = gf + back2
     d_att_b = d_att.astype(BF16)
-    core_copy(0).wait()
-    add_core(0)
-    each(1, 16, lambda d: plane_copy(0, d).start())
+    scatter_plane(0)
 
     def put_pair(at, left, right):
         grads[at : at + C, :] = left[:, 0:128].astype(BF16)
@@ -466,9 +570,8 @@
     grads[SMALL_ROW + 32 : ROWS, :] = jnp.zeros((ROWS - SMALL_ROW - 32, 128), BF16)
     core_copy(1).start()
     din_copies = send_back(1, (d_att + back1).astype(BF16))
-    core_copy(1).wait()
-    add_core(1)
-    each(1, 16, lambda d: plane_copy(1, d).start())
+    scatter_plane(1)
+    scatter_z(0)
 
     hi_iota = lax.broadcasted_iota(jnp.int32, (32, 256), 0)
     lo_iota = lax.broadcasted_iota(jnp.int32, (128, 256), 0)
@@ -489,7 +592,9 @@
             total = total + factors(two(flat, r), [two(values, r) for values in rows])
         return total
 
-    table = lax.fori_loop(0, TOK // 8, pairs, jnp.zeros((HEADS * 32, 128), F32))
+    table = lax.fori_loop(0, 12, pairs, jnp.zeros((HEADS * 32, 128), F32))
+    scatter_z(1)
+    table = lax.fori_loop(12, TOK // 8, pairs, table)
     flat_tail = jnp.concatenate([index_ref[:, 128:TOK].astype(F32), jnp.zeros((TOK, 112), F32)], 1).T[0:16]
     flat_tail = flat_tail.astype(jnp.int32)
     ds_tail = [dsc[h, :, 128:256].T for h in range(HEADS)]
@@ -509,51 +614,6 @@
             device_id_type=MESH,
         )
 
-    each(1, 32, lambda d: t_copy(d).start())
-
-    each(1, 16, lambda d: plane_copy(0, d).wait())
-    owned[0:64, :] = add_plane(0)
-    each(1, 16, lambda d: plane_copy(1, d).wait())
-    owned[64:OWNED, :] = add_plane(1)
-    for n in range(16):
-        z_out[n] = owned[n * ZROWS : (n + 1) * ZROWS, :]
-
-    def z_copy(d):
-        to = (z + d) % 16
-        return pltpu.make_async_remote_copy(
-            src_ref=z_out.at[to],
-            dst_ref=z_in.at[d],
-            send_sem=zs.at[d],
-            recv_sem=zr.at[d],
-            device_id=(lat, to * 2 + ylo),
-            device_id_type=MESH,
-        )
-
-    def z_gather(d):
-        to = (z + d) % 16
-        return pltpu.make_async_remote_copy(
-            src_ref=z_all.at[z],
-            dst_ref=z_all.at[z],
-            send_sem=zgs.at[d],
-            recv_sem=zgr.at[d],
-            device_id=(lat, to * 2 + ylo),
-            device_id_type=MESH,
-        )
-
-    each(1, 16, lambda d: z_copy(d).start())
-    each(1, 16, lambda d: z_copy(d).wait())
-    total = z_out[z]
-    for d in range(1, 16):
-        total = total + z_in[d]
-    z_all[z] = total
-    each(1, 16, lambda d: z_gather(d).start())
-
-    each(1, 32, lambda d: t_copy(d).wait())
-    t_total = t_out[lon]
-    for d in range(1, 32):
-        t_total = t_total + t_in[d]
-    tgrad_ref[lon] = t_total
-
     def t_gather(d):
         return pltpu.make_async_remote_copy(
             src_ref=tgrad_ref.at[lon],
@@ -564,49 +624,26 @@
             device_id_type=MESH,
         )
 
+    each(1, 32, lambda d: t_copy(d).start())
+    gather_z(0)
+    gather_z(1)
+    each(1, 32, lambda d: t_copy(d).wait())
+    t_total = t_out[lon]
+    for d in range(1, 32):
+        t_total = t_total + t_in[d]
+    tgrad_ref[lon] = t_total
     each(1, 32, lambda d: t_gather(d).start())
-
-    each(1, 16, lambda d: z_gather(d).wait())
-    for n in range(16):
-        owned[n * ZROWS : (n + 1) * ZROWS, :] = z_all[n]
-    full_ref[core, k] = owned[...].astype(BF16)
-
-    def plane_gather(d):
-        return pltpu.make_async_remote_copy(
-            src_ref=full_ref.at[core, k],
-            dst_ref=full_ref.at[core, k],
-            send_sem=ags.at[d],
-            recv_sem=agr.at[d],
-            device_id=plane_device((k + d) % 16),
-            device_id_type=MESH,
-        )
-
-    def forward(d):
-        kk = (k + 16 - d) % 16
-        return pltpu.make_async_remote_copy(
-            src_ref=full_ref.at[core, kk],
-            dst_ref=full_ref.at[core, kk],
-            send_sem=fs.at[d],
-            recv_sem=fr.at[d],
-            device_id=(pair_lat, lon),
-            device_id_type=MESH,
-        )
-
-    each(1, 16, lambda d: plane_gather(d).start())
-    forward(0).start()
-
-    def pass_on(d):
-        plane_gather(d).wait()
-        forward(d).start()
-
-    each(1, 16, pass_on)
-
+    gather_plane(0)
+    gather_plane(1)
     for n, copies, ref in ((0, out_copies, out_ref), (1, din_copies, din_ref)):
         for copy in copies:
             copy.wait()
         ref[...] = dot(place_sel[...], out_stack[n, :, 0:C]).astype(BF16)
-    each(0, 16, lambda d: forward(d).wait())
+    pass_on(0)
+    pass_on(1)
     each(1, 32, lambda d: t_gather(d).wait())
+    for n in range(2):
+        each(0, 16, lambda d: forward(n, d).wait())
 
 
 def final_kernel(
@@ -704,14 +741,42 @@
     vmem = pl.BlockSpec(memory_space=pltpu.VMEM)
     shape = jax.ShapeDtypeStruct
     dma = pltpu.SemaphoreType.DMA
+    hbm = pl.BlockSpec(memory_space=pltpu.HBM)
     send_sel, gather_sel, label_sel, send_out_sel, place_sel = selectors()
     by_tile = lambda field: field.transpose(1, 2, 0, 3)
-    bias, win = pl.pallas_call(
+    fields = (by_tile(grid), by_tile(cotangent), region_ids.transpose(1, 0, 2))
+    table = bias_table.transpose(0, 2, 1, 3)
+    passed = (
+        norm_gain,
+        norm_shift,
+        qkv_weight,
+        qkv_bias,
+        proj_weight,
+        proj_bias,
+        fc1_weight,
+        fc1_bias,
+        fc2_weight.T,
+        fc2_bias,
+        send_out_sel,
+        place_sel,
+    )
+    held = lambda a: pltpu.VMEM(a.shape, a.dtype)
+    bias, win, index, *passed = pl.pallas_call(
         halo_kernel,
-        out_shape=(shape((HEADS, TOK, TOK), F32), shape((2, TOK, 256), BF16)),
-        in_specs=[vmem] * 8,
-        out_specs=(vmem,) * 2,
+        out_shape=(
+            shape((HEADS, TOK, TOK), F32),
+            shape((2, TOK, 256), BF16),
+            shape((TOK, TOK), jnp.int32),
+            *(shape(a.shape, a.dtype) for a in passed),
+        ),
+        in_specs=[hbm] * (8 + PASSED),
+        out_specs=(vmem,) * (3 + PASSED),
         scratch_shapes=[
+            *map(held, fields),
+            held(send_sel),
+            held(label_sel),
+            held(table),
+            held(gather_sel),
             pltpu.VMEM((2, 288, 256), BF16),
             pltpu.VMEM((2, 144, 256), BF16),
             pltpu.VMEM((16, 64), F32),
@@ -721,20 +786,17 @@
             pltpu.VMEM((HEADS, 128, 256), F32),
             dma((3,)),
             dma((3,)),
+            dma((8 + PASSED,)),
         ],
         name="halo_and_bias",
         compiler_params=pltpu.CompilerParams(
             collective_id=0, has_side_effects=True, vmem_limit_bytes=32 * 1024 * 1024
         ),
     )(
-        by_tile(grid),
-        region_ids.transpose(1, 0, 2),
-        by_tile(cotangent),
-        bias_table.transpose(0, 2, 1, 3),
-        pair_index,
-        send_sel,
-        gather_sel,
-        label_sel,
+        *(
+            pltpu.with_memory_space_constraint(a, pltpu.HBM)
+            for a in (*fields, send_sel, label_sel, table, pair_index, gather_sel, *passed)
+        )
     )
     out, din, full, tgrad = pl.pallas_call(
         main_kernel,
@@ -759,10 +821,10 @@
             pltpu.VMEM((768, 128), BF16),
             pltpu.VMEM((16, 64, 128), BF16),
             pltpu.VMEM((16, 48, 128), BF16),
-            pltpu.VMEM((16, ZROWS, 128), F32),
-            pltpu.VMEM((16, ZROWS, 128), F32),
-            pltpu.VMEM((16, ZROWS, 128), F32),
-            pltpu.VMEM((OWNED, 128), F32),
+            pltpu.VMEM((2, 16, 4, 128), F32),
+            pltpu.VMEM((2, 16, 4, 128), F32),
+            pltpu.VMEM((2, 16, 4, 128), F32),
+            pltpu.VMEM((64, 128), F32),
             pltpu.VMEM((32, 6, 128), F32),
             pltpu.VMEM((32, 6, 128), F32),
             dma((2, 3)),
@@ -771,18 +833,18 @@
             dma((2,)),
             dma((2, 16)),
             dma((2, 16)),
-            dma((16,)),
-            dma((16,)),
-            dma((16,)),
-            dma((16,)),
+            dma((2, 16)),
+            dma((2, 16)),
+            dma((2, 16)),
+            dma((2, 16)),
             dma((32,)),
             dma((32,)),
             dma((32,)),
             dma((32,)),
-            dma((16,)),
-            dma((16,)),
-            dma((16,)),
-            dma((16,)),
+            dma((2, 16)),
+            dma((2, 16)),
+            dma((2, 16)),
+            dma((2, 16)),
         ],
         name="window_block",
         compiler_params=pltpu.CompilerParams(
@@ -790,20 +852,10 @@
         ),
     )(
         win,
-        norm_gain,
-        norm_shift,
-        qkv_weight,
-        qkv_bias,
-        proj_weight,
-        proj_bias,
-        fc1_weight,
-        fc1_bias,
-        fc2_weight.T,
-        fc2_bias,
+        *passed[0:10],
         bias,
-        pair_index,
-        send_out_sel,
-        place_sel,
+        index,
+        *passed[10:],
     )
     outs = pl.pallas_call(
         final_kernel,

time: 84.5 us -> 68.8 us (0.81)
  local copies, waits for them, and re-layouts: 11.1 us -> 0 us
  Pallas kernels: 71.9 us -> 67.9 us
    unnamed x42 -> x0, local copies, waits for them, and re-layouts: 11.1 us -> none
    pallas_call x1, Pallas kernels: 52.3 us -> 48.2 us  [on_device(): pl.pallas_call(main_kernel, out_shape=(shape((TOK, C), BF16), shape((TOK,...]
where the time goes in v3:
time: 68.8 us; the launch traced here: 68.6 us
  Pallas kernels  67.9 us (99%)
    pallas_call x1, Pallas kernels, on_device(): pl.pallas_call(main_kernel, out_shape=(shape((TOK, C), BF16), shape((TOK,...  48.2 us
    pallas_call x1, Pallas kernels, on_device(): pl.pallas_call(halo_kernel, out_shape=(shape((HEADS, TOK, TOK), F32), sha...  18.3 us
    pallas_call x1, Pallas kernels, on_device(): pl.pallas_call(final_kernel, out_shape=(shape((6, 12, 2, C), BF16), shape...  1.4 us

profile of v3, /device:TPU:1, one launch (start us, length us, event | category | flops | bytes accessed | tf_op | source)
XLA Modules:
  0.0 68.6 jit_solution(6986716532942610562)
XLA Ops:
  0.7 18.3 %halo_and_bias.1 = (f32[6,144,144]{2,1,0:T(8,128)S(1)}, bf16[2,144,256]{2,1,0:T(8,128)(2,1)S(1)}, s32[144,144]{1,0:T(8,128)S(1)}, f32[2,192]{1,0:T(2,128)S(1)}, ...) custom-call(bf16[6,12,2,192]{3,2,1,0:T(2,128)(2,1)} %bitcast.13, ...), custom_call_target="tpu_custom_call" | custom-call | tf_op jit(solution)/shard_map/halo_and_bias/pallas_call | solution.py:764
  19.0 48.2 %window_block.1 = (bf16[144,192]{1,0:T(8,128)(2,1)S(1)}, bf16[144,192]{1,0:T(8,128)(2,1)S(1)}, bf16[2,16,112,128]{3,2,1,0:T(8,128)(2,1)S(1)}, f32[32,6,128]{2,1,0:T(8,128)S(1)}) custom-call(bf16[2,144,256]{2,1,0:T(8,128)(2,1)S(1)} %get-tuple-element.45.win_ref, f32[2,192]{1,0:T(2,128)S(1)} %get-tuple-element.46.gain_ref, ...), custom_call_target="tpu_custom_call" | custom-call | tf_op jit(solution)/shard_map/window_block/pallas_call | solution.py:801
  67.2 1.4 %outputs.1 = (bf16[6,12,2,192]{3,2,1,0:T(2,128)(2,1)}, bf16[6,12,2,192]{3,2,1,0:T(2,128)(2,1)}, f32[2,192]{1,0:T(2,128)}, f32[2,192]{1,0:T(2,128)}, f32[192,576]...) custom-call(bf16[144,192]{1,0:T(8,128)(2,1)S(1)} %get-tuple-element., ...), custom_call_target="tpu_custom_call" | custom-call | tf_op jit(solution)/shard_map/outputs/pallas_call | solution.py:860

commit v4 on v3

--- a/solution.py
+++ b/solution.py
@@ -32,6 +32,11 @@
 SMALL_ROW = 3456
 CHUNKS = ((0, 64), (2048, 48))
 OWNED = 112
+STEPS = (
+    ((1, 0), (3, 0), (0, 1), (0, 3))
+    + ((1, 1), (1, 3), (3, 1), (3, 3), (2, 0), (0, 2))
+    + ((2, 1), (2, 3), (1, 2), (3, 2), (2, 2))
+)
 PASSED = 12
 
 
@@ -69,9 +74,13 @@
 
 
 def look_up_bias(table_ref, index_ref, bias_ref, tab, idx, idx_t, left):
-    tab[...] = jnp.zeros_like(tab)
     for h in range(HEADS):
-        tab[h : h + 1, 0:NBIAS] = table_ref[0, h]
+        for t in range(NHI):
+            n = min(128, NBIAS - t * 128)
+            row = table_ref[0, h, :, t * 128 : t * 128 + n]
+            if n < 128:
+                row = jnp.concatenate([row, jnp.zeros((1, 128 - n), F32)], 1)
+            tab[t, h] = jnp.broadcast_to(row, (8, 128))
     idx[...] = jnp.zeros_like(idx)
     idx[:, 0:TOK] = index_ref[...]
     tail = idx[:, 128:256].astype(F32).T
@@ -82,13 +91,14 @@
     def look(flat, store):
         lo = flat & 127
         hi = flat >> 7
+        acc = [jnp.zeros((8, 128), F32)] * HEADS
+        for t in range(NHI):
+            here = hi == t
+            for h in range(HEADS):
+                got = jnp.take_along_axis(tab[t, h], lo, axis=1, mode="promise_in_bounds")
+                acc[h] = jnp.where(here, got, acc[h])
         for h in range(HEADS):
-            acc = jnp.zeros((8, 128), F32)
-            for t in range(NHI):
-                row = jnp.broadcast_to(tab[h : h + 1, t * 128 : (t + 1) * 128], (8, 128))
-                got = jnp.take_along_axis(row, lo, axis=1, mode="promise_in_bounds")
-                acc = jnp.where(hi == t, got, acc)
-            store(h, acc)
+            store(h, acc[h])
 
     def body(b, carry):
         at = pl.multiple_of(b * 8, 8)
@@ -276,6 +286,7 @@
     z_out,
     z_in,
     z_all,
+    z_part,
     owned,
     t_out,
     t_in,
@@ -289,6 +300,8 @@
     zr,
     zgs,
     zgr,
+    zps,
+    zpr,
     ts,
     tr,
     tgs,
@@ -315,7 +328,8 @@
 
         lax.fori_loop(first_d, last_d, step, 0)
 
-    each(1, 32, lambda d: greet((lat, (lon + d) % 32)))
+    for first, last in ((10, 23), (1, 10), (23, 32)):
+        each(first, last, lambda d: greet((lat, (lon + d) % 32)))
     each(1, 16, lambda d: greet(plane_device((k + d) % 16)))
     greet((pair_lat, lon))
     greet_halo()
@@ -406,7 +420,6 @@
         grads[FC1_ROW + b * C : FC1_ROW + (b + 1) * C, :] = dot(second_b, d_hidden_b, 0, 0).astype(BF16)
         d_second = d_second + dot(d_hidden_b, w1_ref[:, cols], 1, 1)
 
-    z_out[...] = jnp.zeros_like(z_out)
     core_in = (core_in1, core_in2)
     plane_in = (plane_in1, plane_in2)
 
@@ -433,43 +446,59 @@
             device_id_type=MESH,
         )
 
-    def z_copy(n, d):
-        to = (z + d) % 16
+    def z_device(d):
+        return (lat, ((z + d) % 16) * 2 + ylo)
+
+    def z_copy(d):
         return pltpu.make_async_remote_copy(
-            src_ref=z_out.at[n, to],
-            dst_ref=z_in.at[n, d],
-            send_sem=zs.at[n, d],
-            recv_sem=zr.at[n, d],
-            device_id=(lat, to * 2 + ylo),
+            src_ref=z_out.at[(z + d) % 16],
+            dst_ref=z_in.at[d],
+            send_sem=zs.at[d],
+            recv_sem=zr.at[d],
+            device_id=z_device(d),
             device_id_type=MESH,
         )
 
-    def z_gather(n, d):
-        to = (z + d) % 16
+    def z_gather(d):
         return pltpu.make_async_remote_copy(
-            src_ref=z_all.at[n, z],
-            dst_ref=z_all.at[n, z],
-            send_sem=zgs.at[n, d],
-            recv_sem=zgr.at[n, d],
-            device_id=(lat, to * 2 + ylo),
+            src_ref=z_all.at[z],
+            dst_ref=z_all.at[z],
+            send_sem=zgs.at[d],
+            recv_sem=zgr.at[d],
+            device_id=z_device(d),
+            device_id_type=MESH,
+        )
+
+    def z_share(d):
+        return pltpu.make_async_remote_copy(
+            src_ref=z_part.at[z],
+            dst_ref=z_part.at[z],
+            send_sem=zps.at[d],
+            recv_sem=zpr.at[d],
+            device_id=z_device(d),
             device_id_type=MESH,
         )
 
     def owner_rows(n):
         return slice(0, 64) if n == 0 else slice(64, OWNED)
 
+    x_at, y_at = (lat // 2) % 4, (lat // 8) * 2 + ylo
+
     def plane_gather(n, d):
+        xx, yy = (x_at + STEPS[d][0]) % 4, (y_at + STEPS[d][1]) % 4
         return pltpu.make_async_remote_copy(
             src_ref=full_ref.at[core, k, owner_rows(n)],
             dst_ref=full_ref.at[core, k, owner_rows(n)],
             send_sem=ags.at[n, d],
             recv_sem=agr.at[n, d],
-            device_id=plane_device((k + d) % 16),
+            device_id=(((yy // 2) * 4 + xx) * 2 + core, z * 2 + yy % 2),
             device_id_type=MESH,
         )
 
     def forward(n, d):
-        kk = (k + 16 - d) % 16
+        dx, dy = STEPS[d] if d < 15 else (0, 0)
+        xx, yy = (x_at + 4 - dx) % 4, (y_at + 4 - dy) % 4
+        kk = ((yy // 2) * 4 + xx) * 2 + yy % 2
         return pltpu.make_async_remote_copy(
             src_ref=full_ref.at[core, kk, owner_rows(n)],
             dst_ref=full_ref.at[core, kk, owner_rows(n)],
@@ -486,40 +515,56 @@
         grads[mine, :] = (grads[mine, :].astype(F32) + core_in[n][...].astype(F32)).astype(BF16)
         each(1, 16, lambda d: plane_copy(n, d).start())
 
-    def scatter_z(n):
+    def plane_total(n):
         base, rows = CHUNKS[n]
-        per = rows // 16
         each(1, 16, lambda d: plane_copy(n, d).wait())
         total = grads[pl.ds(pl.multiple_of(base + (core * 16 + k) * rows, 16), rows), :].astype(F32)
         for d in range(1, 16):
             total = total + plane_in[n][d].astype(F32)
+        return total
+
+    def scatter_z():
+        total = plane_total(0)
         for m in range(16):
-            z_out[n, m, 0:per] = total[m * per : (m + 1) * per]
-        each(1, 16, lambda d: z_copy(n, d).start())
-
-    def gather_z(n):
-        each(1, 16, lambda d: z_copy(n, d).wait())
-        total = z_out[n, z]
+            z_out[m] = total[m * 4 : (m + 1) * 4]
+        each(1, 16, lambda d: z_copy(d).start())
+
+    def gather_z():
+        each(1, 16, lambda d: z_copy(d).wait())
+        total = z_out[z]
         for d in range(1, 16):
-            total = total + z_in[n, d]
-        z_all[n, z] = total
-        each(1, 16, lambda d: z_gather(n, d).start())
-
-    def gather_plane(n):
-        per = CHUNKS[n][1] // 16
-        each(1, 16, lambda d: z_gather(n, d).wait())
+            total = total + z_in[d]
+        z_all[z] = total
+        each(1, 16, lambda d: z_gather(d).start())
+
+    def share_z():
+        z_part[z] = plane_total(1).astype(BF16)
+        each(1, 16, lambda d: z_share(d).start())
+
+    def start_plane(n):
+        for d in reversed(range(15)):
+            plane_gather(n, d).start()
+        forward(n, 15).start()
+
+    def gather_plane():
+        each(1, 16, lambda d: z_gather(d).wait())
         for m in range(16):
-            owned[m * per : (m + 1) * per, :] = z_all[n, m, 0:per]
-        full_ref[core, k, owner_rows(n)] = owned[0 : CHUNKS[n][1], :].astype(BF16)
-        each(1, 16, lambda d: plane_gather(n, d).start())
-        forward(n, 0).start()
+            owned[m * 4 : (m + 1) * 4, :] = z_all[m]
+        full_ref[core, k, owner_rows(0)] = owned[...].astype(BF16)
+        start_plane(0)
+
+    def gather_plane_shared():
+        each(1, 16, lambda d: z_share(d).wait())
+        total = z_part[0].astype(F32)
+        for m in range(1, 16):
+            total = total + z_part[m].astype(F32)
+        full_ref[core, k, owner_rows(1)] = total.astype(BF16)
+        start_plane(1)
 
     def pass_on(n):
-        def step(d):
+        for d in range(15):
             plane_gather(n, d).wait()
             forward(n, d).start()
-
-        each(1, 16, step)
 
     pl.semaphore_wait(pltpu.get_barrier_semaphore(), 53)
     core_copy(0).start()
@@ -571,35 +616,40 @@
     core_copy(1).start()
     din_copies = send_back(1, (d_att + back1).astype(BF16))
     scatter_plane(1)
-    scatter_z(0)
-
-    hi_iota = lax.broadcasted_iota(jnp.int32, (32, 256), 0)
-    lo_iota = lax.broadcasted_iota(jnp.int32, (128, 256), 0)
+    scatter_z()
+
+    hi_iota = lax.broadcasted_iota(jnp.int32, (32, 256), 0).astype(F32).astype(BF16)
+    lo_iota = lax.broadcasted_iota(jnp.int32, (128, 256), 0).astype(F32).astype(BF16)
+
+    def spread(row, count):
+        return jnp.concatenate([jnp.broadcast_to(row, (16, row.shape[1])).astype(BF16)] * (count // 16), 0)
 
     def factors(flat, rows):
         width = flat.shape[1]
-        is_hi = hi_iota[:, 0:width] == (flat >> 7)
-        lo_hot = jnp.where(lo_iota[:, 0:width] == (flat & 127), 1.0, 0.0).astype(BF16)
-        left = jnp.concatenate([jnp.where(is_hi, row, 0.0).astype(BF16) for row in rows], 0)
-        return dot(left, lo_hot, 1, 1)
+        is_hi = hi_iota[:, 0:width] == spread((flat >> 7).astype(F32), 32)
+        is_lo = lo_iota[:, 0:width] == spread((flat & 127).astype(F32), 128)
+        zero = jnp.zeros((), BF16)
+        left = jnp.concatenate([jnp.where(is_hi, spread(row, 32), zero) for row in rows], 0)
+        return left, jnp.where(is_lo, jnp.ones((), BF16), zero)
 
     def pairs(b, total):
         block = pl.ds(pl.multiple_of(b * 8, 8), 8)
         flat = index_ref[block, 0:128]
         rows = [dsc[h, block, 0:128] for h in range(HEADS)]
         two = lambda values, r: jnp.concatenate([values[r : r + 1], values[r + 1 : r + 2]], 1)
-        for r in range(0, 8, 2):
-            total = total + factors(two(flat, r), [two(values, r) for values in rows])
-        return total
-
-    table = lax.fori_loop(0, 12, pairs, jnp.zeros((HEADS * 32, 128), F32))
-    scatter_z(1)
-    table = lax.fori_loop(12, TOK // 8, pairs, table)
+        parts = [factors(two(flat, r), [two(values, r) for values in rows]) for r in range(0, 8, 2)]
+        left = jnp.concatenate([part[0] for part in parts], 1)
+        right = jnp.concatenate([part[1] for part in parts], 1)
+        return total + dot(left, right, 1, 1)
+
+    table = lax.fori_loop(0, 10, pairs, jnp.zeros((HEADS * 32, 128), F32))
+    share_z()
+    table = lax.fori_loop(10, TOK // 8, pairs, table)
     flat_tail = jnp.concatenate([index_ref[:, 128:TOK].astype(F32), jnp.zeros((TOK, 112), F32)], 1).T[0:16]
     flat_tail = flat_tail.astype(jnp.int32)
     ds_tail = [dsc[h, :, 128:256].T for h in range(HEADS)]
     for r in range(16):
-        table = table + factors(flat_tail[r : r + 1], [t[r : r + 1] for t in ds_tail])
+        table = table + dot(*factors(flat_tail[r : r + 1], [t[r : r + 1] for t in ds_tail]), 1, 1)
     for n in range(32):
         t_out[n] = table[n * 6 : (n + 1) * 6]
 
@@ -625,16 +675,15 @@
         )
 
     each(1, 32, lambda d: t_copy(d).start())
-    gather_z(0)
-    gather_z(1)
+    gather_z()
     each(1, 32, lambda d: t_copy(d).wait())
     t_total = t_out[lon]
     for d in range(1, 32):
         t_total = t_total + t_in[d]
     tgrad_ref[lon] = t_total
     each(1, 32, lambda d: t_gather(d).start())
-    gather_plane(0)
-    gather_plane(1)
+    gather_plane()
+    gather_plane_shared()
     for n, copies, ref in ((0, out_copies, out_ref), (1, din_copies, din_ref)):
         for copy in copies:
             copy.wait()
@@ -643,7 +692,8 @@
     pass_on(1)
     each(1, 32, lambda d: t_gather(d).wait())
     for n in range(2):
-        each(0, 16, lambda d: forward(n, d).wait())
+        for d in range(16):
+            forward(n, d).wait()
 
 
 def final_kernel(
@@ -780,7 +830,7 @@
             pltpu.VMEM((2, 288, 256), BF16),
             pltpu.VMEM((2, 144, 256), BF16),
             pltpu.VMEM((16, 64), F32),
-            pltpu.VMEM((8, 3328), F32),
+            pltpu.VMEM((NHI, HEADS, 8, 128), F32),
             pltpu.VMEM((TOK, 256), jnp.int32),
             pltpu.VMEM((16, 256), jnp.int32),
             pltpu.VMEM((HEADS, 128, 256), F32),
@@ -821,9 +871,10 @@
             pltpu.VMEM((768, 128), BF16),
             pltpu.VMEM((16, 64, 128), BF16),
             pltpu.VMEM((16, 48, 128), BF16),
-            pltpu.VMEM((2, 16, 4, 128), F32),
-            pltpu.VMEM((2, 16, 4, 128), F32),
-            pltpu.VMEM((2, 16, 4, 128), F32),
+            pltpu.VMEM((16, 4, 128), F32),
+            pltpu.VMEM((16, 4, 128), F32),
+            pltpu.VMEM((16, 4, 128), F32),
+            pltpu.VMEM((16, 48, 128), BF16),
             pltpu.VMEM((64, 128), F32),
             pltpu.VMEM((32, 6, 128), F32),
             pltpu.VMEM((32, 6, 128), F32),
@@ -833,10 +884,12 @@
             dma((2,)),
             dma((2, 16)),
             dma((2, 16)),
-            dma((2, 16)),
-            dma((2, 16)),
-            dma((2, 16)),
-            dma((2, 16)),
+            dma((16,)),
+            dma((16,)),
+            dma((16,)),
+            dma((16,)),
+            dma((16,)),
+            dma((16,)),
             dma((32,)),
             dma((32,)),
             dma((32,)),

time: 68.8 us -> 73.5 us (1.068)
  Pallas kernels: 67.9 us -> 72.6 us
    pallas_call x1, Pallas kernels: 48.2 us -> 52.8 us  [on_device(): pl.pallas_call(main_kernel, out_shape=(shape((TOK, C), BF16), shape((TOK,...]
where the time goes in v4:
time: 73.5 us; the launch traced here: 73.3 us
  Pallas kernels  72.6 us (99%)
    pallas_call x1, Pallas kernels, on_device(): pl.pallas_call(main_kernel, out_shape=(shape((TOK, C), BF16), shape((TOK,...  52.8 us
    pallas_call x1, Pallas kernels, on_device(): pl.pallas_call(halo_kernel, out_shape=(shape((HEADS, TOK, TOK), F32), sha...  18.4 us

profile of v4, /device:TPU:1, one launch (start us, length us, event | category | flops | bytes accessed | tf_op | source)
XLA Modules:
  0.0 73.3 jit_solution(4887548212534999717)
XLA Ops:
  0.7 18.4 %halo_and_bias.1 = (f32[6,144,144]{2,1,0:T(8,128)S(1)}, bf16[2,144,256]{2,1,0:T(8,128)(2,1)S(1)}, s32[144,144]{1,0:T(8,128)S(1)}, f32[2,192]{1,0:T(2,128)S(1)}, ...) custom-call(bf16[6,12,2,192]{3,2,1,0:T(2,128)(2,1)} %bitcast.13, ...), custom_call_target="tpu_custom_call" | custom-call | tf_op jit(solution)/shard_map/halo_and_bias/pallas_call | solution.py:814
  19.0 52.8 %window_block.1 = (bf16[144,192]{1,0:T(8,128)(2,1)S(1)}, bf16[144,192]{1,0:T(8,128)(2,1)S(1)}, bf16[2,16,112,128]{3,2,1,0:T(8,128)(2,1)S(1)}, f32[32,6,128]{2,1,0:T(8,128)S(1)}) custom-call(bf16[2,144,256]{2,1,0:T(8,128)(2,1)S(1)} %get-tuple-element.45.win_ref, f32[2,192]{1,0:T(2,128)S(1)} %get-tuple-element.46.gain_ref, ...), custom_call_target="tpu_custom_call" | custom-call | tf_op jit(solution)/shard_map/window_block/pallas_call | solution.py:851
  71.9 1.4 %outputs.1 = (bf16[6,12,2,192]{3,2,1,0:T(2,128)(2,1)}, bf16[6,12,2,192]{3,2,1,0:T(2,128)(2,1)}, f32[2,192]{1,0:T(2,128)}, f32[2,192]{1,0:T(2,128)}, f32[192,576]...) custom-call(bf16[144,192]{1,0:T(8,128)(2,1)S(1)} %get-tuple-element., ...), custom_call_target="tpu_custom_call" | custom-call | tf_op jit(solution)/shard_map/outputs/pallas_call | solution.py:913

commit v5 on v3

--- a/solution.py
+++ b/solution.py
@@ -32,6 +32,11 @@
 SMALL_ROW = 3456
 CHUNKS = ((0, 64), (2048, 48))
 OWNED = 112
+STEPS = (
+    ((1, 0), (3, 0), (0, 1), (0, 3))
+    + ((1, 1), (1, 3), (3, 1), (3, 3), (2, 0), (0, 2))
+    + ((2, 1), (2, 3), (1, 2), (3, 2), (2, 2))
+)
 PASSED = 12
 
 
@@ -69,9 +74,13 @@
 
 
 def look_up_bias(table_ref, index_ref, bias_ref, tab, idx, idx_t, left):
-    tab[...] = jnp.zeros_like(tab)
     for h in range(HEADS):
-        tab[h : h + 1, 0:NBIAS] = table_ref[0, h]
+        for t in range(NHI):
+            n = min(128, NBIAS - t * 128)
+            row = table_ref[0, h, :, t * 128 : t * 128 + n]
+            if n < 128:
+                row = jnp.concatenate([row, jnp.zeros((1, 128 - n), F32)], 1)
+            tab[t, h] = jnp.broadcast_to(row, (8, 128))
     idx[...] = jnp.zeros_like(idx)
     idx[:, 0:TOK] = index_ref[...]
     tail = idx[:, 128:256].astype(F32).T
@@ -82,13 +91,14 @@
     def look(flat, store):
         lo = flat & 127
         hi = flat >> 7
+        acc = [jnp.zeros((8, 128), F32)] * HEADS
+        for t in range(NHI):
+            here = hi == t
+            for h in range(HEADS):
+                got = jnp.take_along_axis(tab[t, h], lo, axis=1, mode="promise_in_bounds")
+                acc[h] = jnp.where(here, got, acc[h])
         for h in range(HEADS):
-            acc = jnp.zeros((8, 128), F32)
-            for t in range(NHI):
-                row = jnp.broadcast_to(tab[h : h + 1, t * 128 : (t + 1) * 128], (8, 128))
-                got = jnp.take_along_axis(row, lo, axis=1, mode="promise_in_bounds")
-                acc = jnp.where(hi == t, got, acc)
-            store(h, acc)
+            store(h, acc[h])
 
     def body(b, carry):
         at = pl.multiple_of(b * 8, 8)
@@ -315,7 +325,8 @@
 
         lax.fori_loop(first_d, last_d, step, 0)
 
-    each(1, 32, lambda d: greet((lat, (lon + d) % 32)))
+    for first, last in ((10, 23), (1, 10), (23, 32)):
+        each(first, last, lambda d: greet((lat, (lon + d) % 32)))
     each(1, 16, lambda d: greet(plane_device((k + d) % 16)))
     greet((pair_lat, lon))
     greet_halo()
@@ -433,43 +444,49 @@
             device_id_type=MESH,
         )
 
+    def z_device(d):
+        return (lat, ((z + d) % 16) * 2 + ylo)
+
     def z_copy(n, d):
-        to = (z + d) % 16
         return pltpu.make_async_remote_copy(
-            src_ref=z_out.at[n, to],
+            src_ref=z_out.at[n, (z + d) % 16],
             dst_ref=z_in.at[n, d],
             send_sem=zs.at[n, d],
             recv_sem=zr.at[n, d],
-            device_id=(lat, to * 2 + ylo),
+            device_id=z_device(d),
             device_id_type=MESH,
         )
 
     def z_gather(n, d):
-        to = (z + d) % 16
         return pltpu.make_async_remote_copy(
             src_ref=z_all.at[n, z],
             dst_ref=z_all.at[n, z],
             send_sem=zgs.at[n, d],
             recv_sem=zgr.at[n, d],
-            device_id=(lat, to * 2 + ylo),
+            device_id=z_device(d),
             device_id_type=MESH,
         )
 
     def owner_rows(n):
         return slice(0, 64) if n == 0 else slice(64, OWNED)
 
+    x_at, y_at = (lat // 2) % 4, (lat // 8) * 2 + ylo
+
     def plane_gather(n, d):
+        xx, yy = (x_at + STEPS[d][0]) % 4, (y_at + STEPS[d][1]) % 4
         return pltpu.make_async_remote_copy(
             src_ref=full_ref.at[core, k, owner_rows(n)],
             dst_ref=full_ref.at[core, k, owner_rows(n)],
             send_sem=ags.at[n, d],
             recv_sem=agr.at[n, d],
-            device_id=plane_device((k + d) % 16),
+            device_id=(((yy // 2) * 4 + xx) * 2 + core, z * 2 + yy % 2),
             device_id_type=MESH,
         )
 
     def forward(n, d):
-        kk = (k + 16 - d) % 16
+        dx, dy = STEPS[d] if d < 15 else (0, 0)
+        xx, yy = (x_at + 4 - dx) % 4, (y_at + 4 - dy) % 4
+        kk = ((yy // 2) * 4 + xx) * 2 + yy % 2
         return pltpu.make_async_remote_copy(
             src_ref=full_ref.at[core, kk, owner_rows(n)],
             dst_ref=full_ref.at[core, kk, owner_rows(n)],
@@ -486,13 +503,17 @@
         grads[mine, :] = (grads[mine, :].astype(F32) + core_in[n][...].astype(F32)).astype(BF16)
         each(1, 16, lambda d: plane_copy(n, d).start())
 
-    def scatter_z(n):
+    def plane_total(n):
         base, rows = CHUNKS[n]
-        per = rows // 16
         each(1, 16, lambda d: plane_copy(n, d).wait())
         total = grads[pl.ds(pl.multiple_of(base + (core * 16 + k) * rows, 16), rows), :].astype(F32)
         for d in range(1, 16):
             total = total + plane_in[n][d].astype(F32)
+        return total
+
+    def scatter_z(n):
+        per = CHUNKS[n][1] // 16
+        total = plane_total(n)
         for m in range(16):
             z_out[n, m, 0:per] = total[m * per : (m + 1) * per]
         each(1, 16, lambda d: z_copy(n, d).start())
@@ -506,31 +527,26 @@
         each(1, 16, lambda d: z_gather(n, d).start())
 
     def gather_plane(n):
-        per = CHUNKS[n][1] // 16
+        rows = CHUNKS[n][1]
+        per = rows // 16
         each(1, 16, lambda d: z_gather(n, d).wait())
         for m in range(16):
             owned[m * per : (m + 1) * per, :] = z_all[n, m, 0:per]
-        full_ref[core, k, owner_rows(n)] = owned[0 : CHUNKS[n][1], :].astype(BF16)
-        each(1, 16, lambda d: plane_gather(n, d).start())
-        forward(n, 0).start()
+        full_ref[core, k, owner_rows(n)] = owned[0:rows, :].astype(BF16)
+        for d in reversed(range(15)):
+            plane_gather(n, d).start()
+        forward(n, 15).start()
 
     def pass_on(n):
-        def step(d):
+        for d in range(15):
             plane_gather(n, d).wait()
             forward(n, d).start()
-
-        each(1, 16, step)
-
-    pl.semaphore_wait(pltpu.get_barrier_semaphore(), 53)
-    core_copy(0).start()
-    out_copies = send_back(0, result)
 
     back2, dgain1, dshift1 = norm_back(d_second, hat2, inv2, gain1)
     keep(2, dgain1)
     keep(6, dshift1)
     d_att = gf + back2
     d_att_b = d_att.astype(BF16)
-    scatter_plane(0)
 
     def put_pair(at, left, right):
         grads[at : at + C, :] = left[:, 0:128].astype(BF16)
@@ -568,38 +584,48 @@
     keep(4, dshift0)
     grads[SMALL_ROW : SMALL_ROW + 32, :] = small[...].astype(BF16)
     grads[SMALL_ROW + 32 : ROWS, :] = jnp.zeros((ROWS - SMALL_ROW - 32, 128), BF16)
+    pl.semaphore_wait(pltpu.get_barrier_semaphore(), 53)
+    core_copy(0).start()
     core_copy(1).start()
+    out_copies = send_back(0, result)
+    scatter_plane(0)
     din_copies = send_back(1, (d_att + back1).astype(BF16))
     scatter_plane(1)
-    scatter_z(0)
-
-    hi_iota = lax.broadcasted_iota(jnp.int32, (32, 256), 0)
-    lo_iota = lax.broadcasted_iota(jnp.int32, (128, 256), 0)
+
+    hi_iota = lax.broadcasted_iota(jnp.int32, (32, 256), 0).astype(F32).astype(BF16)
+    lo_iota = lax.broadcasted_iota(jnp.int32, (128, 256), 0).astype(F32).astype(BF16)
+
+    def spread(row, count):
+        return jnp.concatenate([jnp.broadcast_to(row, (16, row.shape[1])).astype(BF16)] * (count // 16), 0)
 
     def factors(flat, rows):
         width = flat.shape[1]
-        is_hi = hi_iota[:, 0:width] == (flat >> 7)
-        lo_hot = jnp.where(lo_iota[:, 0:width] == (flat & 127), 1.0, 0.0).astype(BF16)
-        left = jnp.concatenate([jnp.where(is_hi, row, 0.0).astype(BF16) for row in rows], 0)
-        return dot(left, lo_hot, 1, 1)
+        is_hi = hi_iota[:, 0:width] == spread((flat >> 7).astype(F32), 32)
+        is_lo = lo_iota[:, 0:width] == spread((flat & 127).astype(F32), 128)
+        zero = jnp.zeros((), BF16)
+        left = jnp.concatenate([jnp.where(is_hi, spread(row, 32), zero) for row in rows], 0)
+        return left, jnp.where(is_lo, jnp.ones((), BF16), zero)
 
     def pairs(b, total):
         block = pl.ds(pl.multiple_of(b * 8, 8), 8)
         flat = index_ref[block, 0:128]
         rows = [dsc[h, block, 0:128] for h in range(HEADS)]
         two = lambda values, r: jnp.concatenate([values[r : r + 1], values[r + 1 : r + 2]], 1)
-        for r in range(0, 8, 2):
-            total = total + factors(two(flat, r), [two(values, r) for values in rows])
-        return total
-
-    table = lax.fori_loop(0, 12, pairs, jnp.zeros((HEADS * 32, 128), F32))
+        parts = [factors(two(flat, r), [two(values, r) for values in rows]) for r in range(0, 8, 2)]
+        left = jnp.concatenate([part[0] for part in parts], 1)
+        right = jnp.concatenate([part[1] for part in parts], 1)
+        return total + dot(left, right, 1, 1)
+
+    table = lax.fori_loop(0, 11, pairs, jnp.zeros((HEADS * 32, 128), F32))
+    scatter_z(0)
+    table = lax.fori_loop(11, 14, pairs, table)
     scatter_z(1)
-    table = lax.fori_loop(12, TOK // 8, pairs, table)
+    table = lax.fori_loop(14, TOK // 8, pairs, table)
     flat_tail = jnp.concatenate([index_ref[:, 128:TOK].astype(F32), jnp.zeros((TOK, 112), F32)], 1).T[0:16]
     flat_tail = flat_tail.astype(jnp.int32)
     ds_tail = [dsc[h, :, 128:256].T for h in range(HEADS)]
     for r in range(16):
-        table = table + factors(flat_tail[r : r + 1], [t[r : r + 1] for t in ds_tail])
+        table = table + dot(*factors(flat_tail[r : r + 1], [t[r : r + 1] for t in ds_tail]), 1, 1)
     for n in range(32):
         t_out[n] = table[n * 6 : (n + 1) * 6]
 
@@ -643,7 +669,8 @@
     pass_on(1)
     each(1, 32, lambda d: t_gather(d).wait())
     for n in range(2):
-        each(0, 16, lambda d: forward(n, d).wait())
+        for d in range(16):
+            forward(n, d).wait()
 
 
 def final_kernel(
@@ -780,7 +807,7 @@
             pltpu.VMEM((2, 288, 256), BF16),
             pltpu.VMEM((2, 144, 256), BF16),
             pltpu.VMEM((16, 64), F32),
-            pltpu.VMEM((8, 3328), F32),
+            pltpu.VMEM((NHI, HEADS, 8, 128), F32),
             pltpu.VMEM((TOK, 256), jnp.int32),
             pltpu.VMEM((16, 256), jnp.int32),
             pltpu.VMEM((HEADS, 128, 256), F32),

time: 68.8 us -> 67.9 us (0.987)
  Pallas kernels: 67.9 us -> 67.1 us
    pallas_call x1, Pallas kernels: 48.2 us -> 47.3 us  [on_device(): pl.pallas_call(main_kernel, out_shape=(shape((TOK, C), BF16), shape((TOK,...]
where the time goes in v5:
time: 67.9 us; the launch traced here: 67.7 us
  Pallas kernels  67.1 us (99%)
    pallas_call x1, Pallas kernels, on_device(): pl.pallas_call(main_kernel, out_shape=(shape((TOK, C), BF16), shape((TOK,...  47.3 us
    pallas_call x1, Pallas kernels, on_device(): pl.pallas_call(halo_kernel, out_shape=(shape((HEADS, TOK, TOK), F32), sha...  18.4 us
    pallas_call x1, Pallas kernels, on_device(): pl.pallas_call(final_kernel, out_shape=(shape((6, 12, 2, C), BF16), shape...  1.4 us

profile of v5, /device:TPU:1, one launch (start us, length us, event | category | flops | bytes accessed | tf_op | source)
XLA Modules:
  0.0 67.7 jit_solution(10209557789579908648)
XLA Ops:
  0.7 18.4 %halo_and_bias.1 = (f32[6,144,144]{2,1,0:T(8,128)S(1)}, bf16[2,144,256]{2,1,0:T(8,128)(2,1)S(1)}, s32[144,144]{1,0:T(8,128)S(1)}, f32[2,192]{1,0:T(2,128)S(1)}, ...) custom-call(bf16[6,12,2,192]{3,2,1,0:T(2,128)(2,1)} %bitcast.13, ...), custom_call_target="tpu_custom_call" | custom-call | tf_op jit(solution)/shard_map/halo_and_bias/pallas_call | solution.py:791
  19.0 47.3 %window_block.1 = (bf16[144,192]{1,0:T(8,128)(2,1)S(1)}, bf16[144,192]{1,0:T(8,128)(2,1)S(1)}, bf16[2,16,112,128]{3,2,1,0:T(8,128)(2,1)S(1)}, f32[32,6,128]{2,1,0:T(8,128)S(1)}) custom-call(bf16[2,144,256]{2,1,0:T(8,128)(2,1)S(1)} %get-tuple-element.45.win_ref, f32[2,192]{1,0:T(2,128)S(1)} %get-tuple-element.46.gain_ref, ...), custom_call_target="tpu_custom_call" | custom-call | tf_op jit(solution)/shard_map/window_block/pallas_call | solution.py:828
  66.3 1.4 %outputs.1 = (bf16[6,12,2,192]{3,2,1,0:T(2,128)(2,1)}, bf16[6,12,2,192]{3,2,1,0:T(2,128)(2,1)}, f32[2,192]{1,0:T(2,128)}, f32[2,192]{1,0:T(2,128)}, f32[192,576]...) custom-call(bf16[144,192]{1,0:T(8,128)(2,1)S(1)} %get-tuple-element., ...), custom_call_target="tpu_custom_call" | custom-call | tf_op jit(solution)/shard_map/outputs/pallas_call | solution.py:887

commit v6 on v5

--- a/solution.py
+++ b/solution.py
@@ -121,10 +121,18 @@
         bias_ref[h, :, 128:TOK] = left[h].T[0:TOK, 0:16]
 
 
+def rem(a, b):
+    return lax.rem(a, b)
+
+
+def half(a):
+    return lax.div(a, 2)
+
+
 def around():
     lat = lax.axis_index("lat")
     lon = lax.axis_index("lon")
-    return lat, lon, (lat + 1) % 16, (lat + 15) % 16, (lon + 1) % 32, (lon + 31) % 32
+    return lat, lon, rem(lat + 1, 16), rem(lat + 15, 16), rem(lon + 1, 32), rem(lon + 31, 32)
 
 
 def greet(device):
@@ -309,25 +317,30 @@
     fr,
 ):
     lat, lon, lat_up, lat_dn, lon_up, lon_dn = around()
-    core = lat % 2
+    core = rem(lat, 2)
     pair_lat = lat + 1 - 2 * core
-    ylo = lon % 2
-    z = lon // 2
-    k = (lat // 2) * 2 + ylo
+    ylo = rem(lon, 2)
+    z = half(lon)
+    k = half(lat) * 2 + ylo
 
     def plane_device(kk):
-        return ((kk // 2) * 2 + core, z * 2 + kk % 2)
+        return (half(kk) * 2 + core, z * 2 + rem(kk, 2))
 
     def each(first_d, last_d, body):
         def step(d, carry):
             body(d)
             return carry
 
-        lax.fori_loop(first_d, last_d, step, 0)
-
-    for first, last in ((10, 23), (1, 10), (23, 32)):
-        each(first, last, lambda d: greet((lat, (lon + d) % 32)))
-    each(1, 16, lambda d: greet(plane_device((k + d) % 16)))
+        lax.fori_loop(first_d, last_d, step, 0, unroll=True)
+
+    def far_first(count, body):
+        first, last = count // 2 - 3, count // 2 + 4
+        each(first, last, body)
+        each(1, first, body)
+        each(last, count, body)
+
+    far_first(32, lambda d: greet((lat, rem(lon + d, 32))))
+    each(1, 16, lambda d: greet(plane_device(rem(k + d, 16))))
     greet((pair_lat, lon))
     greet_halo()
 
@@ -434,7 +447,7 @@
 
     def plane_copy(n, d):
         base, rows = CHUNKS[n]
-        kk = (k + d) % 16
+        kk = rem(k + d, 16)
         return pltpu.make_async_remote_copy(
             src_ref=grads.at[pl.ds(pl.multiple_of(base + (core * 16 + kk) * rows, 16), rows), :],
             dst_ref=plane_in[n].at[d],
@@ -445,11 +458,11 @@
         )
 
     def z_device(d):
-        return (lat, ((z + d) % 16) * 2 + ylo)
+        return (lat, rem(z + d, 16) * 2 + ylo)
 
     def z_copy(n, d):
         return pltpu.make_async_remote_copy(
-            src_ref=z_out.at[n, (z + d) % 16],
+            src_ref=z_out.at[n, rem(z + d, 16)],
             dst_ref=z_in.at[n, d],
             send_sem=zs.at[n, d],
             recv_sem=zr.at[n, d],
@@ -470,23 +483,23 @@
     def owner_rows(n):
         return slice(0, 64) if n == 0 else slice(64, OWNED)
 
-    x_at, y_at = (lat // 2) % 4, (lat // 8) * 2 + ylo
+    x_at, y_at = rem(half(lat), 4), lax.div(lat, 8) * 2 + ylo
 
     def plane_gather(n, d):
-        xx, yy = (x_at + STEPS[d][0]) % 4, (y_at + STEPS[d][1]) % 4
+        xx, yy = rem(x_at + STEPS[d][0], 4), rem(y_at + STEPS[d][1], 4)
         return pltpu.make_async_remote_copy(
             src_ref=full_ref.at[core, k, owner_rows(n)],
             dst_ref=full_ref.at[core, k, owner_rows(n)],
             send_sem=ags.at[n, d],
             recv_sem=agr.at[n, d],
-            device_id=(((yy // 2) * 4 + xx) * 2 + core, z * 2 + yy % 2),
+            device_id=((half(yy) * 4 + xx) * 2 + core, z * 2 + rem(yy, 2)),
             device_id_type=MESH,
         )
 
     def forward(n, d):
         dx, dy = STEPS[d] if d < 15 else (0, 0)
-        xx, yy = (x_at + 4 - dx) % 4, (y_at + 4 - dy) % 4
-        kk = ((yy // 2) * 4 + xx) * 2 + yy % 2
+        xx, yy = rem(x_at + 4 - dx, 4), rem(y_at + 4 - dy, 4)
+        kk = (half(yy) * 4 + xx) * 2 + rem(yy, 2)
         return pltpu.make_async_remote_copy(
             src_ref=full_ref.at[core, kk, owner_rows(n)],
             dst_ref=full_ref.at[core, kk, owner_rows(n)],
@@ -516,7 +529,7 @@
         total = plane_total(n)
         for m in range(16):
             z_out[n, m, 0:per] = total[m * per : (m + 1) * per]
-        each(1, 16, lambda d: z_copy(n, d).start())
+        far_first(16, lambda d: z_copy(n, d).start())
 
     def gather_z(n):
         each(1, 16, lambda d: z_copy(n, d).wait())
@@ -524,7 +537,7 @@
         for d in range(1, 16):
             total = total + z_in[n, d]
         z_all[n, z] = total
-        each(1, 16, lambda d: z_gather(n, d).start())
+        far_first(16, lambda d: z_gather(n, d).start())
 
     def gather_plane(n):
         rows = CHUNKS[n][1]
@@ -572,6 +585,8 @@
         dk = dk + dot(ds_b, only(h, q), 0, 0)
         dv = dv + dot(p.astype(BF16), dm_h, 0, 0)
     dq_b, dk_b, dv_b = dq.astype(BF16), dk.astype(BF16), dv.astype(BF16)
+    pl.semaphore_wait(pltpu.get_barrier_semaphore(), 53)
+    core_copy(0).start()
     put_pair(QP_ROW, dot(first_b, dq_b, 0, 0), dot(first_b, dk_b, 0, 0))
     put_pair(QP_ROW + 3 * C, dot(first_b, dv_b, 0, 0), dw_proj)
     d_bias = jnp.concatenate(
@@ -584,13 +599,11 @@
     keep(4, dshift0)
     grads[SMALL_ROW : SMALL_ROW + 32, :] = small[...].astype(BF16)
     grads[SMALL_ROW + 32 : ROWS, :] = jnp.zeros((ROWS - SMALL_ROW - 32, 128), BF16)
-    pl.semaphore_wait(pltpu.get_barrier_semaphore(), 53)
-    core_copy(0).start()
     core_copy(1).start()
+    scatter_plane(0)
+    scatter_plane(1)
     out_copies = send_back(0, result)
-    scatter_plane(0)
     din_copies = send_back(1, (d_att + back1).astype(BF16))
-    scatter_plane(1)
 
     hi_iota = lax.broadcasted_iota(jnp.int32, (32, 256), 0).astype(F32).astype(BF16)
     lo_iota = lax.broadcasted_iota(jnp.int32, (128, 256), 0).astype(F32).astype(BF16)
@@ -630,7 +643,7 @@
         t_out[n] = table[n * 6 : (n + 1) * 6]
 
     def t_copy(d):
-        to = (lon + d) % 32
+        to = rem(lon + d, 32)
         return pltpu.make_async_remote_copy(
             src_ref=t_out.at[to],
             dst_ref=t_in.at[d],
@@ -646,11 +659,11 @@
             dst_ref=tgrad_ref.at[lon],
             send_sem=tgs.at[d],
             recv_sem=tgr.at[d],
-            device_id=(lat, (lon + d) % 32),
+            device_id=(lat, rem(lon + d, 32)),
             device_id_type=MESH,
         )
 
-    each(1, 32, lambda d: t_copy(d).start())
+    far_first(32, lambda d: t_copy(d).start())
     gather_z(0)
     gather_z(1)
     each(1, 32, lambda d: t_copy(d).wait())
@@ -658,7 +671,7 @@
     for d in range(1, 32):
         t_total = t_total + t_in[d]
     tgrad_ref[lon] = t_total
-    each(1, 32, lambda d: t_gather(d).start())
+    far_first(32, lambda d: t_gather(d).start())
     gather_plane(0)
     gather_plane(1)
     for n, copies, ref in ((0, out_copies, out_ref), (1, din_copies, din_ref)):

time: 67.9 us -> 66.5 us (0.979)
  Pallas kernels: 67.1 us -> 65.6 us
    pallas_call x1, Pallas kernels: 47.3 us -> 45.9 us  [on_device(): pl.pallas_call(main_kernel, out_shape=(shape((TOK, C), BF16), shape((TOK,...]
where the time goes in v6:
time: 66.5 us; the launch traced here: 66.3 us
  Pallas kernels  65.6 us (99%)
  between operations  0.67 us (1%)
    pallas_call x1, Pallas kernels, on_device(): pl.pallas_call(main_kernel, out_shape=(shape((TOK, C), BF16), shape((TOK,...  45.9 us
    pallas_call x1, Pallas kernels, on_device(): pl.pallas_call(halo_kernel, out_shape=(shape((HEADS, TOK, TOK), F32), sha...  18.4 us
    pallas_call x1, Pallas kernels, on_device(): pl.pallas_call(final_kernel, out_shape=(shape((6, 12, 2, C), BF16), shape...  1.4 us

profile of v6, /device:TPU:1, one launch (start us, length us, event | category | flops | bytes accessed | tf_op | source)
XLA Modules:
  0.0 66.3 jit_solution(14652851285878036559)
XLA Ops:
  0.7 18.4 %halo_and_bias.1 = (f32[6,144,144]{2,1,0:T(8,128)S(1)}, bf16[2,144,256]{2,1,0:T(8,128)(2,1)S(1)}, s32[144,144]{1,0:T(8,128)S(1)}, f32[2,192]{1,0:T(2,128)S(1)}, ...) custom-call(bf16[6,12,2,192]{3,2,1,0:T(2,128)(2,1)} %bitcast.13, ...), custom_call_target="tpu_custom_call" | custom-call | tf_op jit(solution)/shard_map/halo_and_bias/pallas_call | solution.py:804
  19.0 45.9 %window_block.1 = (bf16[144,192]{1,0:T(8,128)(2,1)S(1)}, bf16[144,192]{1,0:T(8,128)(2,1)S(1)}, bf16[2,16,112,128]{3,2,1,0:T(8,128)(2,1)S(1)}, f32[32,6,128]{2,1,0:T(8,128)S(1)}) custom-call(bf16[2,144,256]{2,1,0:T(8,128)(2,1)S(1)} %get-tuple-element.45.win_ref, f32[2,192]{1,0:T(2,128)S(1)} %get-tuple-element.46.gain_ref, ...), custom_call_target="tpu_custom_call" | custom-call | tf_op jit(solution)/shard_map/window_block/pallas_call | solution.py:841
  64.9 1.4 %outputs.1 = (bf16[6,12,2,192]{3,2,1,0:T(2,128)(2,1)}, bf16[6,12,2,192]{3,2,1,0:T(2,128)(2,1)}, f32[2,192]{1,0:T(2,128)}, f32[2,192]{1,0:T(2,128)}, f32[192,576]...) custom-call(bf16[144,192]{1,0:T(8,128)(2,1)S(1)} %get-tuple-element., ...), custom_call_target="tpu_custom_call" | custom-call | tf_op jit(solution)/shard_map/outputs/pallas_call | solution.py:900
